TPU v7x, 512 devices: a whole 4x4x16 slice. The times are simulated.
512 devices in a mesh: slab: 64 (over z, x), tile: 8 (over y, core).
Axes of the slice: x: 4, y: 4, z: 16, core: 2. Of those that a mesh axis runs over, the one named last changes fastest.
Arguments:
- images: float32 [256, 2048, 256], P('slab', 'tile'), may hold values from -36 to 36
- tissue_mask: int32 [256, 32, 4], P('slab', 'tile'), may hold values 0 or 1
Outputs:
- flow_field: float32 [2, 256, 32, 4], P(None, 'slab', 'tile')
- mesh_shift: float32 [2, 256, 32, 4], P(None, 'slab', 'tile')
All inputs are finite; a program needn't handle non-finite values. No bound on the sum of `tissue_mask` on one device may be relied on, other than what follows from the above.
Results may differ from a plain program's by a relative error of at most 0.0003.
Values sent between devices are 32-bit elements; how exact they have to be, the bound alone decides.
A program may use at most 128 MiB of HBM per device.

v0:
```python
import jax
import jax.numpy as jnp
from jax import lax
from jax.sharding import PartitionSpec as P

PATCH = 128
STRIDE = 64
TEMP = 256
STEPS = 4
RIM = 32


inter_stiff = 1.0
plane_stiff = 0.25
step_size = 0.5
norm_eps = 1e-06
highest = lax.Precision.HIGHEST


def passed_along(block, axis, distance):
    devices = range(lax.axis_size(axis))
    route = [(i - distance, i) for i in devices if i - distance in devices]
    return lax.ppermute(block, axis, route)


def padded(x, sides, width):
    for axis, dim in sides:
        count, length = (lax.axis_size(axis), x.shape[dim])
        up = [(i, (i + 1) % count) for i in range(count - 1)]
        down = [(j, i) for i, j in up]
        last = lax.slice_in_dim(x, length - width, length, axis=dim)
        initial = lax.slice_in_dim(x, 0, width, axis=dim)
        before = lax.ppermute(last, axis, up)
        after = lax.ppermute(initial, axis, down)
        x = jnp.concatenate([before, x, after], axis=dim)
    return x


def dft_tables(length):
    index = jnp.arange(length)
    phase = (index[:, None] * index[None, :] % length).astype(jnp.float32) * (2.0 * jnp.pi / length)
    return (jnp.cos(phase), jnp.sin(phase))


def from_left(table, batch):
    return jnp.einsum("kn,bnm->bkm", table, batch, precision=highest)


def from_right(batch, table):
    return jnp.einsum("bkn,nm->bkm", batch, table, precision=highest)


def spectrum(pieces, cosine, sine):
    half_real = from_left(cosine, pieces)
    half_imag = -from_left(sine, pieces)
    real_part = from_right(half_real, cosine) + from_right(half_imag, sine)
    imag_part = from_right(half_imag, cosine) - from_right(half_real, sine)
    return (real_part, imag_part)


def soft_flow(earlier, later, cosine, sine, lags):
    cross_real = earlier[0] * later[0] + earlier[1] * later[1]
    cross_imag = earlier[0] * later[1] - earlier[1] * later[0]
    inner_real = from_left(cosine, cross_real) - from_left(sine, cross_imag)
    inner_imag = from_left(cosine, cross_imag) + from_left(sine, cross_real)
    length = cosine.shape[0]
    corr = (from_right(inner_real, cosine) - from_right(inner_imag, sine)) / (length * length)
    scores = corr / TEMP
    top = jnp.max(scores, axis=(-2, -1), keepdims=True)
    weights = jnp.exp(scores - top)
    total = jnp.sum(weights, axis=(-2, -1))
    flow_rows = jnp.sum(weights * lags[:, None], axis=(-2, -1)) / total
    flow_cols = jnp.sum(weights * lags[None, :], axis=(-2, -1)) / total
    return jnp.stack([flow_rows, flow_cols])


def forces(ghosted, springs_wide):
    center = ghosted[:, 1:-1, 1:-1]
    before = ghosted[:, :-2, 1:-1]
    after = ghosted[:, 2:, 1:-1]
    stretch = springs_wide[2, 1:-1, 1:-1] * (center - before - springs_wide[:2, 1:-1, 1:-1])
    stretch_next = springs_wide[2, 2:, 1:-1] * (after - center - springs_wide[:2, 2:, 1:-1])
    sideways = jnp.pad(center, ((0, 0), (0, 0), (0, 0), (1, 1)))
    beside_all = (
        ghosted[:, 1:-1, :-2] + ghosted[:, 1:-1, 2:] + sideways[..., :-2] + sideways[..., 2:]
    )
    return inter_stiff * (stretch_next - stretch) + plane_stiff * (beside_all - 4.0 * center)


def step_scale(force_own, count):
    total = lax.psum(jnp.sum(force_own * force_own), ("slab", "tile"))
    return step_size / jnp.sqrt(total / count + norm_eps)


def local(images, tissue_mask):
    sec_dev, tile_rows, columns = images.shape
    before = passed_along(images[-1:], "slab", 1)
    stacked = jnp.concatenate([before, images], axis=0)
    rimmed = padded(stacked, (("tile", 1),), RIM)
    rimmed = jnp.pad(rimmed, ((0, 0), (0, 0), (RIM, RIM)))
    node_rows = tile_rows // STRIDE
    node_cols = columns // STRIDE
    cosine, sine = dft_tables(PATCH)
    index = jnp.arange(PATCH)
    lags = jnp.where(index < PATCH // 2, index, index - PATCH).astype(jnp.float32)

    def row_flows(row):
        band = lax.dynamic_slice_in_dim(rimmed, row * STRIDE, PATCH, 1)
        pieces = jnp.stack(
            [band[:, :, j * STRIDE : j * STRIDE + PATCH] for j in range(node_cols)], axis=1
        )
        earlier = spectrum(pieces[0], cosine, sine)
        results = []
        for later_index in range(sec_dev):
            later = spectrum(pieces[later_index + 1], cosine, sine)
            results.append(soft_flow(earlier, later, cosine, sine, lags))
            earlier = later
        return jnp.stack(results, axis=1)

    per_row = lax.map(row_flows, jnp.arange(node_rows))
    flow_field = jnp.transpose(per_row, (1, 2, 0, 3))
    global_first = lax.axis_index("slab") * sec_dev + jnp.arange(sec_dev)
    live = (global_first > 0).astype(jnp.float32)
    flow_field = flow_field * live[None, :, None, None]
    spring = tissue_mask.astype(jnp.float32) * live[:, None, None]
    springs = jnp.concatenate([flow_field, spring[None]], axis=0)
    count = 2 * sec_dev * node_rows * node_cols * lax.axis_size("slab") * lax.axis_size("tile")
    mesh = jnp.zeros((2, sec_dev, node_rows, node_cols), jnp.float32)
    above = passed_along(springs[:, :1], "slab", -1)
    springs_wide = jnp.concatenate([jnp.zeros_like(springs[:, :1]), springs, above], axis=1)
    springs_wide = jnp.pad(springs_wide, ((0, 0), (0, 0), (1, 1), (0, 0)))
    for step in range(STEPS):
        ghosted = padded(mesh, (("slab", 1), ("tile", 2)), 1)
        force = forces(ghosted, springs_wide)
        mesh = mesh + step_scale(force, count) * force
    return (flow_field, mesh)


def solution(mesh):
    placed = (P("slab", "tile", None), P("slab", "tile", None))
    return jax.shard_map(
        local,
        mesh=mesh,
        in_specs=placed,
        out_specs=(P(None, "slab", "tile", None), P(None, "slab", "tile", None)),
        check_vma=False,
    )
```

profile of v0, /device:TPU:1, one launch (start us, length us, event | category | flops | bytes accessed | tf_op | source)
XLA Modules:
  0.0 707.2 jit_solution(11936288504806909070)
XLA Ops:
  0.7 4.1 collective-permute-start.5
  4.7 1.3 collective-permute-start.4
  6.0 1.0 slice.233
  7.0 4.0 collective-permute-start
  11.0 0.8 fusion.482
  11.8 2.5 collective-permute-done
  14.5 6.3 collective-permute-start.1
  20.8 2.3 collective-permute-start.2
  23.4 4.0 collective-permute-done.2
  27.6 1.8 copy.97
  29.4 1.7 pad.21.clone
  31.1 184.0 %while.15 = (s32[]{:T(128)}, f32[4,2,4,4]{2,3,0,1:T(4,128)S(1)}, s32[4]{0:T(128)S(1)}, f32[5,320,320]{1,2,0:T(8,128)S(1)}, s32[]{:T(128)}, /*index=5*/s32[1]{0:T...) while((s32[]{:T(128)}, f32[4,2,4,4]{2,3,0,1:T(4,128)S(1)}, s32[4]{0:T(128)S(1)}, ...), condition=%wide.region_17.18_spmd.clone.clone, body=%wide.region_0.17_spmd.clone.clone.sunk | while | flops 5454627328 | bytes 44575588 | solution.py:120
  76.6 0.8 multiply_subtract_fusion.5
  115.7 0.8 multiply_subtract_fusion.5
  154.8 0.8 multiply_subtract_fusion.5
  193.8 0.8 multiply_subtract_fusion.5
  215.1 1.3 collective-permute-start.3
  216.4 1.9 collective-permute-start.6
  218.4 2.4 collective-permute-start.7
  220.9 2.4 collective-permute-done.7
  223.3 0.7 multiply_reduce_fusion.11
  224.0 113.9 %psum.28 = f32[]{:T(128)} all-reduce(f32[]{:T(128)} %get-tuple-element.424), channel_id=1, replica_groups=mesh['slab'=64,'tile'=8] {'slab','tile'}, use_global_device_ids=true, to_apply=%region_19.20 | all-reduce | flops 1 | bytes 8 | tf_op jit(solution)/shard_map/psum | solution.py:91
  338.7 2.2 collective-permute-start.9
  341.0 1.3 collective-permute-start.8
  342.3 3.2 collective-permute-done.8
  345.6 3.3 collective-permute-start.10
  348.9 2.0 collective-permute-start.11
  350.9 2.9 collective-permute-done.11
  353.8 0.7 multiply_reduce_fusion.10
  354.5 106.5 %psum.29 = f32[]{:T(128)} all-reduce(f32[]{:T(128)} %get-tuple-element.422), channel_id=1, replica_groups=mesh['slab'=64,'tile'=8] {'slab','tile'}, use_global_device_ids=true, to_apply=%region_21.22 | all-reduce | flops 1 | bytes 8 | tf_op jit(solution)/shard_map/psum | solution.py:91
  461.8 2.8 collective-permute-start.13
  464.6 1.3 collective-permute-start.12
  465.9 3.2 collective-permute-done.12
  469.2 3.3 collective-permute-start.14
  472.5 2.0 collective-permute-start.15
  474.5 2.9 collective-permute-done.15
  477.4 0.7 multiply_reduce_fusion.9
  478.2 105.0 %psum.30 = f32[]{:T(128)} all-reduce(f32[]{:T(128)} %get-tuple-element.420), channel_id=1, replica_groups=mesh['slab'=64,'tile'=8] {'slab','tile'}, use_global_device_ids=true, to_apply=%region_23.24 | all-reduce | flops 1 | bytes 8 | tf_op jit(solution)/shard_map/psum | solution.py:91
  584.0 3.1 collective-permute-start.17
  587.0 1.3 collective-permute-start.16
  588.4 3.2 collective-permute-done.16
  591.6 3.3 collective-permute-start.18
  594.9 2.0 collective-permute-start.19
  596.9 0.7 copy.61
  597.6 2.2 collective-permute-done.19
  599.8 0.7 multiply_reduce_fusion.8
  600.6 105.0 %psum.31 = f32[]{:T(128)} all-reduce(f32[]{:T(128)} %get-tuple-element.418), channel_id=1, replica_groups=mesh['slab'=64,'tile'=8] {'slab','tile'}, use_global_device_ids=true, to_apply=%region_25.26 | all-reduce | flops 1 | bytes 8 | tf_op jit(solution)/shard_map/psum | solution.py:91
  706.3 0.7 copy.62
  (313 shorter events, 149.9 us)
Async XLA Ops:
  0.6 13.7 %copy-start = (f32[4,256,256]{2,1,0:T(8,128)S(1)}, f32[4,256,256]{2,1,0:T(8,128)}, u32[]{:S(2)}) copy-start(f32[4,256,256]{2,1,0:T(8,128)} %param.4) | copy-start | bytes 3145732
  0.7 22.7 %collective-permute-start.5 = (f32[2,1,4,4]{1,3,2,0:T(4,128)S(1)}, f32[2,1,4,4]{1,3,2,0:T(4,128)S(1)}, u32[]{:S(2)}, u32[]{:S(2)}) collective-permute-start(f32[2,1,4,4]{1,3,2,0:T(4,128)S(1)} %broadcast.89), channel_id=1, source_target_pairs={{0,8},{8,16},{16,24},{24,32},{32,40},{40,48},{48,56},{56,64},{64,7... | collective-permute-start | bytes 392 | tf_op jit(solution)/shard_map/ppermute | solution.py:33
  4.7 18.6 %collective-permute-start.4 = (f32[2,1,4,4]{1,3,2,0:T(4,128)S(1)}, f32[2,1,4,4]{1,3,2,0:T(4,128)S(1)}, u32[]{:S(2)}, u32[]{:S(2)}) collective-permute-start(f32[2,1,4,4]{1,3,2,0:T(4,128)S(1)} %broadcast.89), channel_id=1, source_target_pairs={{8,0},{16,8},{24,16},{32,24},{40,32},{48,40},{56,48},{64,56},{72,6... | collective-permute-start | bytes 392 | tf_op jit(solution)/shard_map/ppermute | solution.py:34
  7.0 7.3 %collective-permute-start = (f32[1,256,256]{2,1,0:T(8,128)S(1)}, f32[1,256,256]{2,1,0:T(8,128)S(1)}, u32[]{:S(2)}, u32[]{:S(2)}) collective-permute-start(f32[1,256,256]{2,1,0:T(8,128)S(1)} %slice.233), channel_id=1, source_target_pairs={{0,8},{8,16},{16,24},{24,32},{32,40},{40,48},{48,56},{56,64},{64,7... | collective-permute-start | bytes 786440 | tf_op jit(solution)/shard_map/ppermute | solution.py:23
  14.3 8.7 %copy-start.1 = (s32[4,4,4]{2,1,0:T(4,128)S(1)}, s32[4,4,4]{2,1,0:T(4,128)}, u32[]{:S(2)}) copy-start(s32[4,4,4]{2,1,0:T(4,128)} %param.5) | copy-start | bytes 772
  14.5 9.0 %collective-permute-start.1 = (f32[5,32,256]{2,1,0:T(8,128)S(1)}, f32[5,32,256]{2,1,0:T(8,128)S(1)}, u32[]{:S(2)}, u32[]{:S(2)}) collective-permute-start(f32[5,32,256]{2,1,0:T(8,128)S(1)} %get-tuple-element.464), channel_id=1, source_target_pairs={{0,1},{1,2},{2,3},{3,4},{4,5},{5,6},{6,7},{8,9},{9,10},{10,11},{11... | collective-permute-start | bytes 491528 | tf_op jit(solution)/shard_map/ppermute | solution.py:33
  20.8 6.6 collective-permute-start.2
  215.1 5.6 collective-permute-start.3
  216.4 4.4 collective-permute-start.6
  218.4 4.9 collective-permute-start.7
  338.7 3.6 collective-permute-start.9
  341.0 4.5 collective-permute-start.8
  345.6 5.3 collective-permute-start.10
  348.9 4.9 collective-permute-start.11
  461.8 4.1 collective-permute-start.13
  464.6 4.5 collective-permute-start.12
  469.2 5.3 collective-permute-start.14
  472.5 4.9 collective-permute-start.15
  584.0 4.4 collective-permute-start.17
  587.0 4.5 collective-permute-start.16
  591.6 6.0 collective-permute-start.18
  594.9 4.9 collective-permute-start.19
where the time goes:
time: 710 us; the launch traced here: 707 us
  blocking collectives  430 us (61%)
  matrix products  145 us (20%)
  starting transfers between devices  51.4 us (7%)
  loops' own time  32.2 us (5%)
  waiting for transfers between devices  26.4 us (4%)
  local copies, waits for them, and re-layouts  11 us (2%)
  other arithmetic  7.19 us (1%)
    psum x4, blocking collectives, step_scale(): total = lax.psum(jnp.sum(force_own * force_own), ('slab', 'tile'))  430 us
    dot_general x112, matrix products, from_right(): return jnp.einsum('bkn,nm->bkm', batch, table, precision=highest)  79.2 us
    dot_general x104, matrix products, from_left(): return jnp.einsum('kn,bnm->bkm', table, batch, precision=highest)  65.3 us
    another operation x1, loops' own time, local(): per_row = lax.map(row_flows, jnp.arange(node_rows))  32.2 us
    ppermute x9, starting transfers between devices, padded(): before = lax.ppermute(last, axis, up)  30.3 us
    ppermute x9, waiting for transfers between devices, padded(): after = lax.ppermute(initial, axis, down)  23.9 us
    ppermute x9, starting transfers between devices, padded(): after = lax.ppermute(initial, axis, down)  15.8 us
  transfers between devices with their start and end apart: 20, of which 9 were waited for; matrix products, arithmetic and copies ran while one was open for 0% of the time, Pallas kernels for 0%

commit v1 on v0

v1 whole, which is shorter than its diff:
```python
import functools

import jax
import jax.numpy as jnp
import ml_dtypes
import numpy as np
from jax import lax
from jax.experimental import pallas as pl
from jax.experimental.pallas import tpu as pltpu
from jax.sharding import PartitionSpec as P

MESH = pl.DeviceIdType.MESH
PATCH = 128
STRIDE = 64
HALF = 64
RIM = 32
TEMP = 256
STEPS = 4
COLS = 256
NODES = 4
SEC = 4
ROWS = 256
WIDE = ROWS + 2 * RIM
LANES = 128

inter_stiff = 1.0
plane_stiff = 0.25
step_size = 0.5
norm_eps = 1e-06

f32 = jnp.float32
bf16 = jnp.bfloat16


def pieces(table):
    high = table.astype(np.float32).astype(ml_dtypes.bfloat16)
    low = (table - high.astype(np.float64)).astype(np.float32).astype(ml_dtypes.bfloat16)
    return high, low


def tables():
    k = np.arange(HALF)[:, None]
    x = np.arange(PATCH)[None, :]
    angle = 2.0 * np.pi * ((k * x) % PATCH) / PATCH
    cosine, sine = np.cos(angle), np.sin(angle)
    alternate = np.where(np.arange(PATCH) % 2 == 0, 1.0, -1.0)
    columns = np.zeros((COLS, 2, NODES, HALF))
    sine_slots = sine.copy()
    sine_slots[0] = alternate
    for j in range(NODES):
        for y in range(PATCH):
            col = j * STRIDE - RIM + y
            if 0 <= col < COLS:
                columns[col, 0, j] = cosine[:, y]
                columns[col, 1, j] = sine_slots[:, y]
    columns = columns.reshape(COLS, 2 * NODES * HALF)
    zero = np.zeros(PATCH)
    rows = np.zeros((4, HALF, 2, PATCH))
    rows[0, :, 0], rows[0, :, 1] = cosine, -sine
    rows[1, :, 0], rows[1, :, 1] = sine, cosine
    rows[2, :, 0], rows[2, :, 1] = cosine, sine
    rows[3, :, 0], rows[3, :, 1] = sine, -cosine
    rows[0, 0] = np.stack([zero + 1.0, zero])
    rows[1, 0] = np.stack([zero, zero + 1.0])
    rows[2, 0] = np.stack([alternate, zero])
    rows[3, 0] = np.stack([zero, alternate])
    back = np.zeros((2, PATCH, 4, HALF))
    for part, (c_part, s_part) in enumerate(((cosine, -sine), (sine, cosine), (cosine, sine), (sine, -cosine))):
        back[0, :, part] = c_part.T
        back[1, :, part] = s_part.T
    back[:, :, :, 0] = 0.0
    back[0, :, 0, 0] = 1.0
    back[1, :, 1, 0] = 1.0
    back[0, :, 2, 0] = alternate
    back[1, :, 3, 0] = alternate
    rows = rows.reshape(4 * HALF, 2 * PATCH)
    back = back.reshape(2 * PATCH, 4 * HALF)
    unit = np.log2(np.e) / (PATCH * PATCH * TEMP)
    cos_out, sin_out = 2.0 * unit * cosine, 2.0 * unit * sine_slots
    cos_out[0] = 0.25 * unit
    sin_out[0] = 0.25 * unit * alternate
    final = np.zeros((2, 2, HALF, 2, PATCH))
    for j in range(2):
        final[0, j, :, j] = cos_out
        final[1, j, :, j] = sin_out
    final = final.reshape(4 * HALF, 2 * PATCH)
    return [piece for table in (columns, rows, back, final) for piece in pieces(table)]


def split(x):
    high = x.astype(bf16)
    low = (x - high.astype(f32)).astype(bf16)
    return high, low


def dot(a, b):
    return jnp.dot(a, b, preferred_element_type=f32)


def dot3(a, b):
    return dot(a[0], b[0]) + dot(a[0], b[1]) + dot(a[1], b[0])


def iota(shape, dim):
    return lax.broadcasted_iota(jnp.int32, shape, dim)


def kernel(
    slabs,
    tiles,
    x_count,
    images,
    mask,
    cols_h,
    cols_l,
    rows_h,
    rows_l,
    back_h,
    back_l,
    last_h,
    last_l,
    flow_out,
    mesh_out,
    buf,
    z_h,
    z_l,
    spec,
    tops,
    sums,
    outgo,
    income,
    part,
    heard,
    local_sem,
    img_send,
    img_recv,
    halo_send,
    halo_recv,
    sum_send,
    sum_recv,
):
    z_count = slabs // x_count
    p = lax.axis_index("slab")
    t = lax.axis_index("tile")
    p_next, p_back = lax.rem(p + 1, slabs), lax.rem(p + slabs - 1, slabs)
    t_next, t_back = lax.rem(t + 1, tiles), lax.rem(t + tiles - 1, tiles)
    px, pz = lax.rem(p, x_count), lax.div(p, x_count)
    around = [(a, b) for a in (p_back, p, p_next) for b in (t_back, t, t_next)]
    around = [(n, d) for n, d in enumerate(around) if n != 4]

    def others(phase):
        if phase == 0:
            return [(p, lax.rem(t + d, tiles)) for d in range(1, tiles)]
        if phase == 1:
            return [(pz * x_count + lax.rem(px + d, x_count), t) for d in range(1, x_count)]
        return [(lax.rem(pz + d, z_count) * x_count + px, t) for d in range(1, z_count)]

    partners = [d for _, d in around] + [d for phase in range(3) for d in others(phase)]

    own = pltpu.make_async_copy(images, buf.at[pl.ds(1, SEC), pl.ds(RIM, ROWS), :], local_sem)
    own.start()
    barrier = pltpu.get_barrier_semaphore()
    for device in partners:
        pl.semaphore_signal(barrier, inc=1, device_id=device, device_id_type=MESH)
    pl.semaphore_wait(barrier, len(partners))

    top_rim, bottom_rim, middle = pl.ds(0, RIM), pl.ds(RIM + ROWS, RIM), pl.ds(RIM, ROWS)
    first_rows, last_rows = pl.ds(0, RIM), pl.ds(ROWS - RIM, RIM)
    sections = pl.ds(1, SEC)
    moves = [
        (images.at[:, last_rows, :], buf.at[sections, top_rim, :], (p, t_next)),
        (images.at[:, first_rows, :], buf.at[sections, bottom_rim, :], (p, t_back)),
        (images.at[pl.ds(SEC - 1, 1)], buf.at[pl.ds(0, 1), middle, :], (p_next, t)),
        (images.at[pl.ds(SEC - 1, 1), last_rows, :], buf.at[pl.ds(0, 1), top_rim, :], (p_next, t_next)),
        (images.at[pl.ds(SEC - 1, 1), first_rows, :], buf.at[pl.ds(0, 1), bottom_rim, :], (p_next, t_back)),
    ]
    copies = [
        pltpu.make_async_remote_copy(
            src_ref=src,
            dst_ref=dst,
            send_sem=img_send.at[n],
            recv_sem=img_recv.at[n],
            device_id=device,
            device_id_type=MESH,
        )
        for n, (src, dst, device) in enumerate(moves)
    ]
    for copy in copies:
        copy.start()

    def transform_columns(s, start, count):
        x_h, x_l = split(buf[s, pl.ds(start, count), :])
        z = dot(x_h, cols_h[...]) + dot(x_l, cols_h[...]) + dot(x_h, cols_l[...])
        high, low = split(z)
        z_h[s, pl.ds(start, count), :] = high
        z_l[s, pl.ds(start, count), :] = low

    def transform_rims(s):
        @pl.when(t == 0)
        def _():
            buf[s, top_rim, :] = jnp.zeros((RIM, COLS), f32)

        @pl.when(t == tiles - 1)
        def _():
            buf[s, bottom_rim, :] = jnp.zeros((RIM, COLS), f32)

        transform_columns(s, 0, RIM)
        transform_columns(s, RIM + ROWS, RIM)

    own.wait()

    @pl.loop(1, SEC + 1)
    def _(s):
        transform_columns(s, RIM, ROWS)

    copies[0].wait()
    copies[1].wait()

    @pl.loop(1, SEC + 1)
    def _(s):
        transform_rims(s)

    slot = lax.rem(iota((HALF, COLS), 1), HALF)
    inner_rows = iota((HALF, COLS), 0) > 0
    edge = (slot == 0) & inner_rows
    corner = (iota((8, COLS), 0) == 0) & (lax.rem(iota((8, COLS), 1), HALF) == 0)
    lag = iota((PATCH, 1), 0)
    lag = jnp.where(lag < PATCH // 2, lag, lag - PATCH).astype(f32)

    def quarters(x):
        return [x[n * HALF : (n + 1) * HALF] for n in range(4)]

    def spectrum(s, i):
        rows = pl.ds(i * STRIDE, PATCH)
        stacked = [
            jnp.concatenate([z[s, rows, :COLS], z[s, rows, COLS:]], axis=0) for z in (z_h, z_l)
        ]
        full = dot3((rows_h[...], rows_l[...]), stacked)
        a, b, c, d = quarters(full)
        spec[s, i, 0:HALF] = jnp.where(edge, a + c, a)
        spec[s, i, HALF : 2 * HALF] = jnp.where(edge, b + d, b)
        spec[s, i, 2 * HALF : 3 * HALF] = jnp.where(edge, b - d, c)
        spec[s, i, 3 * HALF :] = jnp.where(edge, c - a, d)

    def patched(general, special):
        return jnp.concatenate([jnp.where(corner, special, general[:8]), general[8:]], axis=0)

    def pair(earlier, i):
        ap, aq, ar, at = quarters(spec[earlier, i])
        bp, bq, br, bt = quarters(spec[earlier + 1, i])
        xp = patched(ap * bp + aq * bq, 4.0 * ap[:8] * bp[:8])
        xq = patched(ap * bq - aq * bp, 4.0 * aq[:8] * bq[:8])
        xr = patched(ar * br + at * bt, 4.0 * ar[:8] * br[:8])
        xt = patched(ar * bt - at * br, 4.0 * at[:8] * bt[:8])
        cross = jnp.concatenate(
            [
                jnp.where(edge, xp - xt, xp),
                jnp.where(edge, xq + xr, xq),
                jnp.where(edge, xp + xt, xr),
                jnp.where(edge, xq - xr, xt),
            ],
            axis=0,
        )
        u = split(dot3((back_h[...], back_l[...]), split(cross)))
        for half in range(2):
            lanes = slice(half * LANES, (half + 1) * LANES)
            u_h, u_l = (jnp.concatenate([x[:PATCH, lanes], x[PATCH:, lanes]], axis=1) for x in u)
            scores = dot(u_h, last_h[...]) + dot(u_l, last_h[...]) + dot(u_h, last_l[...])
            top = jnp.max(scores, axis=0, keepdims=True)
            weights = jnp.exp2(scores - top)
            total = jnp.sum(weights, axis=0, keepdims=True)
            moment = jnp.sum(weights * lag, axis=0, keepdims=True)
            place = slice(half * COLS, (half + 1) * COLS)
            tops[i, pl.ds(earlier, 1), place] = top
            tops[i, pl.ds(earlier + SEC, 1), place] = top
            sums[i, pl.ds(earlier, 1), place] = total
            sums[i, pl.ds(earlier + SEC, 1), place] = moment

    @pl.loop(0, SEC + 1)
    def _(m):
        s = lax.rem(m + 1, SEC + 1)

        @pl.when(m == SEC)
        def _():
            for copy in copies[2:]:
                copy.wait()
            transform_columns(0, RIM, ROWS)
            transform_rims(0)

        for i in range(NODES):
            spectrum(s, i)

        @pl.when(m > 0)
        def _():
            for i in range(NODES):
                pair(lax.rem(m, SEC), i)

    lane8 = iota((8, LANES), 1)
    row8 = iota((8, LANES), 0)
    lag_cols = jnp.where(lane8 < PATCH // 2, lane8, lane8 - PATCH).astype(f32)
    tile = jnp.zeros((8, LANES), f32)
    for i in range(NODES):
        for j in range(NODES):
            lanes = slice(j * LANES, (j + 1) * LANES)
            top = tops[i, :, lanes]
            scaled = sums[i, :, lanes] * jnp.exp2(top - jnp.max(top, axis=1, keepdims=True))
            both = jnp.sum(scaled, axis=1, keepdims=True)
            across = jnp.sum(scaled * lag_cols, axis=1, keepdims=True)
            total = both[:SEC]
            node = i * NODES + j
            flow_rows = jnp.concatenate([both[SEC:] / total, jnp.zeros((SEC, 1), f32)], axis=0)
            flow_cols = jnp.concatenate([across[:SEC] / total, jnp.zeros((SEC, 1), f32)], axis=0)
            tile = jnp.where(lane8 == node, flow_rows, tile)
            tile = jnp.where(lane8 == HALF + node, flow_cols, tile)
    live = (row8 % SEC + p > 0).astype(f32)
    spring = jnp.zeros((SEC, LANES), f32)
    for i in range(NODES):
        here = jnp.concatenate([mask[s, i : i + 1, :] for s in range(SEC)], axis=0).astype(f32)
        here = jnp.concatenate([here, jnp.zeros((SEC, LANES - NODES), f32)], axis=1)
        spring = spring + (pltpu.roll(here, i * NODES, 1) if i else here)
    spring = jnp.concatenate([jnp.zeros((SEC, LANES), f32), spring], axis=0)
    spring = spring + pltpu.roll(spring, HALF, 1)
    tile = (tile + spring) * live

    def write(out, x, shift):
        for c in range(2):
            for i in range(NODES):
                offset = (c * HALF + shift + i * NODES) % LANES
                moved = pltpu.roll(x, LANES - offset, 1) if offset else x
                for s in range(SEC):
                    out[c, s, i : i + 1, :] = moved[s : s + 1, :NODES]

    for n in range(3):
        outgo[n] = pltpu.roll(tile, 16 * n, 1) if n else tile
    halo = []
    for n, device in around:
        copy = pltpu.make_async_remote_copy(
            src_ref=outgo.at[2 - n % 3],
            dst_ref=income.at[8 - n],
            send_sem=halo_send.at[n],
            recv_sem=halo_recv.at[8 - n],
            device_id=device,
            device_id_type=MESH,
        )
        copy.start()
        halo.append(copy)
    write(flow_out, tile, 0)
    for copy in halo:
        copy.wait()

    blocks = []
    t_low, t_high = (t > 0).astype(f32), (t < tiles - 1).astype(f32)
    p_low, p_high = (p > 0).astype(f32), (p < slabs - 1).astype(f32)
    for a, there in enumerate((p_low, 1.0, p_high)):
        centre = outgo[1] if a == 1 else income[3 * a + 1]
        blocks.append(there * (t_low * income[3 * a] + centre + t_high * income[3 * a + 2]))
    zeros4 = jnp.zeros((SEC, LANES), f32)
    flow = jnp.concatenate([b[:SEC] for b in blocks] + [zeros4], axis=0)
    spring = jnp.concatenate([b[SEC:] for b in blocks] + [zeros4], axis=0)
    wide = 4 * SEC
    lane = lax.rem(iota((wide, LANES), 1), HALF)
    node_row, node_col = lax.div(lane, NODES), lax.rem(lane, NODES)
    inside = (node_row < 3 * NODES) & ((node_row >= NODES) | (t > 0)) & ((node_row < 2 * NODES) | (t < tiles - 1))
    inside = inside.astype(f32)
    has_left, has_right = (node_col > 0).astype(f32), (node_col < NODES - 1).astype(f32)

    def differ(stretch):
        return inter_stiff * (pltpu.roll(stretch, wide - 1, 0) - stretch)

    def apply(v):
        stretch = spring * (v - pltpu.roll(v, 1, 0))
        beside = (
            pltpu.roll(v, NODES, 1)
            + pltpu.roll(v, LANES - NODES, 1)
            + has_left * pltpu.roll(v, 1, 1)
            + has_right * pltpu.roll(v, LANES - 1, 1)
        )
        return inside * (differ(stretch) + plane_stiff * (beside - 4.0 * v))

    powers = [differ(-spring * flow)]
    for _ in range(STEPS - 1):
        powers.append(apply(powers[-1]))
    mine = ((row8 >= SEC) & (lax.rem(lane8, HALF) >= 16) & (lax.rem(lane8, HALF) < 32)).astype(f32)
    cores = [v[:8] * mine for v in powers]
    grams = [(a, b) for a in range(STEPS) for b in range(a, STEPS)]
    packed = [jnp.sum(cores[a] * cores[b], axis=0, keepdims=True) for a, b in grams]
    value = jnp.concatenate(packed + [jnp.zeros((16 - len(grams), LANES), f32)], axis=0)

    base = 0
    for phase in range(3):
        devices = others(phase)
        if not devices:
            continue
        part[phase] = value
        sent = []
        for n, device in enumerate(devices):
            copy = pltpu.make_async_remote_copy(
                src_ref=part.at[phase],
                dst_ref=heard.at[base + n],
                send_sem=sum_send.at[base + n],
                recv_sem=sum_recv.at[base + n],
                device_id=device,
                device_id_type=MESH,
            )
            copy.start()
            sent.append(copy)
        for copy in sent:
            copy.wait()
        for n in range(len(devices)):
            value = value + heard[base + n]
        base += len(devices)

    totals = jnp.sum(value, axis=1, keepdims=True)
    gram = {}
    for n, (a, b) in enumerate(grams):
        gram[a, b] = gram[b, a] = totals[n : n + 1, :]
    count = 2 * SEC * NODES * NODES * slabs * tiles
    zero = jnp.zeros((1, 1), f32)
    force = [zero + 1.0, zero, zero, zero]
    moved = [zero] * STEPS
    for step in range(STEPS):
        square = zero
        for a in range(step + 1):
            square = square + force[a] * force[a] * gram[a, a]
            for b in range(a + 1, step + 1):
                square = square + 2.0 * force[a] * force[b] * gram[a, b]
        scale = step_size / jnp.sqrt(jnp.maximum(square, 0.0) / count + norm_eps)
        moved = [m + scale * f for m, f in zip(moved, force)]
        force = [f + (scale * force[n - 1] if n else 0.0) for n, f in enumerate(force)]
    mesh_shift = sum(m * v[SEC : 2 * SEC] for m, v in zip(moved, powers))
    write(mesh_out, mesh_shift, 16)


def local(slabs, tiles, images, tissue_mask):
    x_count = 4 if slabs % 4 == 0 else slabs
    group = tiles - 1 + x_count - 1 + slabs // x_count - 1
    vmem = pl.BlockSpec(memory_space=pltpu.VMEM)
    constants = tables()
    out = jax.ShapeDtypeStruct((2, SEC, NODES, NODES), f32)
    dma = pltpu.SemaphoreType.DMA
    return pl.pallas_call(
        functools.partial(kernel, slabs, tiles, x_count),
        out_shape=(out, out),
        in_specs=[pl.BlockSpec(memory_space=pl.ANY), vmem] + [vmem] * len(constants),
        out_specs=(vmem, vmem),
        scratch_shapes=[
            pltpu.VMEM((SEC + 1, WIDE, COLS), f32),
            pltpu.VMEM((SEC + 1, WIDE, 2 * COLS), bf16),
            pltpu.VMEM((SEC + 1, WIDE, 2 * COLS), bf16),
            pltpu.VMEM((SEC + 1, NODES, 4 * HALF, COLS), f32),
            pltpu.VMEM((NODES, 2 * SEC, NODES * LANES), f32),
            pltpu.VMEM((NODES, 2 * SEC, NODES * LANES), f32),
            pltpu.VMEM((3, 8, LANES), f32),
            pltpu.VMEM((9, 8, LANES), f32),
            pltpu.VMEM((3, 16, LANES), f32),
            pltpu.VMEM((group, 16, LANES), f32),
            dma,
            dma((5,)),
            dma((5,)),
            dma((9,)),
            dma((9,)),
            dma((group,)),
            dma((group,)),
        ],
        compiler_params=pltpu.CompilerParams(
            collective_id=0, has_side_effects=True, vmem_limit_bytes=48 * 1024 * 1024
        ),
    )(images, tissue_mask, *[jnp.asarray(c) for c in constants])


def solution(mesh):
    placed = (P("slab", "tile", None), P("slab", "tile", None))
    return jax.shard_map(
        functools.partial(local, mesh.shape["slab"], mesh.shape["tile"]),
        mesh=mesh,
        in_specs=placed,
        out_specs=(P(None, "slab", "tile", None), P(None, "slab", "tile", None)),
        check_vma=False,
    )
```

time: 710 us -> 66 us (0.09)
  the two profiles are of different devices: /device:TPU:1 before, /device:TPU:2 now
where the time goes in v1:
time: 66 us; the launch traced here: 65.6 us
  Pallas kernels  54.5 us (83%)
  local copies, waits for them, and re-layouts  10.4 us (16%)
  between operations  0.66 us (1%)
    pallas_call x1, Pallas kernels, local(): pl.pallas_call(functools.partial(kernel, slabs, tiles, x_count), out_shap...  54.5 us
    unnamed x22, local copies, waits for them, and re-layouts  10.4 us

profile of v1, /device:TPU:2, one launch (start us, length us, event | category | flops | bytes accessed | tf_op | source)
XLA Modules:
  0.0 65.6 jit_solution(12220740588852908386)
XLA Ops:
  0.6 0.0 copy-start
  0.6 1.2 %copy-done = f32[4,256,256]{2,1,0:T(8,128)S(1)} copy-done((f32[4,256,256]{2,1,0:T(8,128)S(1)}, f32[4,256,256]{2,1,0:T(8,128)}, u32[]{:S(2)}) %copy-start) | copy-done | bytes 1048600
  1.9 0.0 copy-start.1
  1.9 0.9 %copy-done.1 = bf16[256,512]{1,0:T(8,128)(2,1)S(1)} copy-done((bf16[256,512]{1,0:T(8,128)(2,1)S(1)}, bf16[256,512]{1,0:T(8,128)(2,1)}, u32[]{:S(2)}) %copy-start.1) | copy-done | bytes 262168
  2.8 0.0 copy-start.2
  2.8 0.9 %copy-done.2 = bf16[256,512]{1,0:T(8,128)(2,1)S(1)} copy-done((bf16[256,512]{1,0:T(8,128)(2,1)S(1)}, bf16[256,512]{1,0:T(8,128)(2,1)}, u32[]{:S(2)}) %copy-start.2) | copy-done | bytes 262168
  3.8 0.0 copy-start.3
  3.8 0.9 %copy-done.3 = bf16[256,256]{1,0:T(8,128)(2,1)S(1)} copy-done((bf16[256,256]{1,0:T(8,128)(2,1)S(1)}, bf16[256,256]{1,0:T(8,128)(2,1)}, u32[]{:S(2)}) %copy-start.3) | copy-done | bytes 131096
  4.7 0.0 copy-start.4
  4.7 0.9 %copy-done.4 = bf16[256,256]{1,0:T(8,128)(2,1)S(1)} copy-done((bf16[256,256]{1,0:T(8,128)(2,1)S(1)}, bf16[256,256]{1,0:T(8,128)(2,1)}, u32[]{:S(2)}) %copy-start.4) | copy-done | bytes 131096
  5.6 0.0 copy-start.5
  5.6 0.9 %copy-done.5 = bf16[256,256]{1,0:T(8,128)(2,1)S(1)} copy-done((bf16[256,256]{1,0:T(8,128)(2,1)S(1)}, bf16[256,256]{1,0:T(8,128)(2,1)}, u32[]{:S(2)}) %copy-start.5) | copy-done | bytes 131096
  6.5 0.0 copy-start.6
  6.5 0.9 %copy-done.6 = bf16[256,256]{1,0:T(8,128)(2,1)S(1)} copy-done((bf16[256,256]{1,0:T(8,128)(2,1)S(1)}, bf16[256,256]{1,0:T(8,128)(2,1)}, u32[]{:S(2)}) %copy-start.6) | copy-done | bytes 131096
  7.4 0.0 copy-start.7
  7.4 0.9 %copy-done.7 = bf16[256,256]{1,0:T(8,128)(2,1)S(1)} copy-done((bf16[256,256]{1,0:T(8,128)(2,1)S(1)}, bf16[256,256]{1,0:T(8,128)(2,1)}, u32[]{:S(2)}) %copy-start.7) | copy-done | bytes 131096
  8.3 0.0 copy-start.8
  8.3 0.9 %copy-done.8 = bf16[256,256]{1,0:T(8,128)(2,1)S(1)} copy-done((bf16[256,256]{1,0:T(8,128)(2,1)S(1)}, bf16[256,256]{1,0:T(8,128)(2,1)}, u32[]{:S(2)}) %copy-start.8) | copy-done | bytes 131096
  9.2 0.0 copy-start.9
  9.2 0.7 %copy-done.9 = s32[4,4,4]{2,1,0:T(4,128)S(1)} copy-done((s32[4,4,4]{2,1,0:T(4,128)S(1)}, s32[4,4,4]{2,1,0:T(4,128)}, u32[]{:S(2)}) %copy-start.9) | copy-done | bytes 280
  9.9 54.5 %shard_map.113 = (f32[2,4,4,4]{3,2,1,0:T(4,128)S(1)}, f32[2,4,4,4]{3,2,1,0:T(4,128)S(1)}) custom-call(f32[4,256,256]{2,1,0:T(8,128)S(1)} %copy-done, s32[4,4,4]{2,1,0:T(4,128)S(1)} %copy-done.9, bf16[256,512]{1,0:T(8,128)(2,1)S(1)} %copy-done.2, bf16[256,512]{1,0:T(8,128)(2,1)S(1)} %copy-done.1, bf16[256,256]{1,0:T(8,128)(2,1)S(1)} %copy-done.8, ...), custom_call_target="tpu_custom_call" | custom-call | tf_op jit(solution)/shard_map/pallas_call | solution.py:441
  64.4 0.6 copy.14
  65.0 0.6 copy.15
Async XLA Ops:
  0.6 1.2 %copy-start = (f32[4,256,256]{2,1,0:T(8,128)S(1)}, f32[4,256,256]{2,1,0:T(8,128)}, u32[]{:S(2)}) copy-start(f32[4,256,256]{2,1,0:T(8,128)} %images.1) | copy-start | bytes 3145732
  1.9 0.9 %copy-start.1 = (bf16[256,512]{1,0:T(8,128)(2,1)S(1)}, bf16[256,512]{1,0:T(8,128)(2,1)}, u32[]{:S(2)}) copy-start(bf16[256,512]{1,0:T(8,128)(2,1)} %constant.17.clone.cols_l) | copy-start | bytes 786436
  2.8 0.9 %copy-start.2 = (bf16[256,512]{1,0:T(8,128)(2,1)S(1)}, bf16[256,512]{1,0:T(8,128)(2,1)}, u32[]{:S(2)}) copy-start(bf16[256,512]{1,0:T(8,128)(2,1)} %constant.16.clone.cols_h) | copy-start | bytes 786436
  3.8 0.9 %copy-start.3 = (bf16[256,256]{1,0:T(8,128)(2,1)S(1)}, bf16[256,256]{1,0:T(8,128)(2,1)}, u32[]{:S(2)}) copy-start(bf16[256,256]{1,0:T(8,128)(2,1)} %constant.23.clone.last_l) | copy-start | bytes 393220
  4.7 0.9 %copy-start.4 = (bf16[256,256]{1,0:T(8,128)(2,1)S(1)}, bf16[256,256]{1,0:T(8,128)(2,1)}, u32[]{:S(2)}) copy-start(bf16[256,256]{1,0:T(8,128)(2,1)} %constant.22.clone.last_h) | copy-start | bytes 393220
  5.6 0.9 %copy-start.5 = (bf16[256,256]{1,0:T(8,128)(2,1)S(1)}, bf16[256,256]{1,0:T(8,128)(2,1)}, u32[]{:S(2)}) copy-start(bf16[256,256]{1,0:T(8,128)(2,1)} %constant.21.clone.back_l) | copy-start | bytes 393220
  6.5 0.9 %copy-start.6 = (bf16[256,256]{1,0:T(8,128)(2,1)S(1)}, bf16[256,256]{1,0:T(8,128)(2,1)}, u32[]{:S(2)}) copy-start(bf16[256,256]{1,0:T(8,128)(2,1)} %constant.20.clone.back_h) | copy-start | bytes 393220
  7.4 0.9 %copy-start.7 = (bf16[256,256]{1,0:T(8,128)(2,1)S(1)}, bf16[256,256]{1,0:T(8,128)(2,1)}, u32[]{:S(2)}) copy-start(bf16[256,256]{1,0:T(8,128)(2,1)} %constant.19.clone.rows_l) | copy-start | bytes 393220
  8.3 0.9 %copy-start.8 = (bf16[256,256]{1,0:T(8,128)(2,1)S(1)}, bf16[256,256]{1,0:T(8,128)(2,1)}, u32[]{:S(2)}) copy-start(bf16[256,256]{1,0:T(8,128)(2,1)} %constant.18.clone.rows_h) | copy-start | bytes 393220
  9.2 0.7 %copy-start.9 = (s32[4,4,4]{2,1,0:T(4,128)S(1)}, s32[4,4,4]{2,1,0:T(4,128)}, u32[]{:S(2)}) copy-start(s32[4,4,4]{2,1,0:T(4,128)} %mask.1) | copy-start | bytes 772

commit v2 on v1

v2 whole, which is shorter than its diff:
```python
import functools

import jax
import jax.numpy as jnp
import ml_dtypes
import numpy as np
from jax import lax
from jax.experimental import pallas as pl
from jax.experimental.pallas import tpu as pltpu
from jax.sharding import PartitionSpec as P

MESH = pl.DeviceIdType.MESH
PATCH = 128
STRIDE = 64
HALF = 64
RIM = 32
TEMP = 256
STEPS = 4
BLOCK = 16
X_COUNT = 4
COLS = 256
NODES = 4
SEC = 4
ROWS = 256
WIDE = ROWS + 2 * RIM
LANES = 128

inter_stiff = 1.0
plane_stiff = 0.25
step_size = 0.5
norm_eps = 1e-06

f32 = jnp.float32
bf16 = jnp.bfloat16


def pieces(table):
    high = table.astype(np.float32).astype(ml_dtypes.bfloat16)
    low = (table - high.astype(np.float64)).astype(np.float32).astype(ml_dtypes.bfloat16)
    return high, low


def tables():
    k = np.arange(HALF)[:, None]
    x = np.arange(PATCH)[None, :]
    angle = 2.0 * np.pi * ((k * x) % PATCH) / PATCH
    cosine, sine = np.cos(angle), np.sin(angle)
    alternate = np.where(np.arange(PATCH) % 2 == 0, 1.0, -1.0)
    columns = np.zeros((COLS, 2, NODES, HALF))
    sine_slots = sine.copy()
    sine_slots[0] = alternate
    for j in range(NODES):
        for y in range(PATCH):
            col = j * STRIDE - RIM + y
            if 0 <= col < COLS:
                columns[col, 0, j] = cosine[:, y]
                columns[col, 1, j] = sine_slots[:, y]
    zero = np.zeros(PATCH)
    rows = np.zeros((4, HALF, 2, PATCH))
    rows[0, :, 0], rows[0, :, 1] = cosine, -sine
    rows[1, :, 0], rows[1, :, 1] = sine, cosine
    rows[2, :, 0], rows[2, :, 1] = cosine, sine
    rows[3, :, 0], rows[3, :, 1] = sine, -cosine
    rows[0, 0] = np.stack([zero + 1.0, zero])
    rows[1, 0] = np.stack([zero, zero + 1.0])
    rows[2, 0] = np.stack([alternate, zero])
    rows[3, 0] = np.stack([zero, alternate])
    back = np.zeros((2, PATCH, 4, HALF))
    for part, (c_part, s_part) in enumerate(((cosine, -sine), (sine, cosine), (cosine, sine), (sine, -cosine))):
        back[0, :, part] = c_part.T
        back[1, :, part] = s_part.T
    back[:, :, :, 0] = 0.0
    back[0, :, 0, 0] = 1.0
    back[1, :, 1, 0] = 1.0
    back[0, :, 2, 0] = alternate
    back[1, :, 3, 0] = alternate
    rows = rows.reshape(4 * HALF, 2 * PATCH)
    back = back.reshape(2 * PATCH, 4 * HALF)
    unit = np.log2(np.e) / (PATCH * PATCH * TEMP)
    cos_out, sin_out = 2.0 * unit * cosine, 2.0 * unit * sine_slots
    cos_out[0] = 0.25 * unit
    sin_out[0] = 0.25 * unit * alternate
    final = np.zeros((2, 2, HALF, 2, PATCH))
    for j in range(2):
        final[0, j, :, j] = cos_out
        final[1, j, :, j] = sin_out
    final = final.reshape(4 * HALF, 2 * PATCH)
    columns = columns.reshape(COLS, 2, NODES * HALF)
    parts = [piece for table in (columns[:, 0], columns[:, 1], rows, back, final) for piece in pieces(table)]
    return np.stack(parts)


def split(x):
    high = x.astype(bf16)
    low = (x - high.astype(f32)).astype(bf16)
    return high, low


def dot(a, b):
    return jnp.dot(a, b, preferred_element_type=f32)


def dot3(a, b):
    return dot(a[0], b[0]) + dot(a[0], b[1]) + dot(a[1], b[0])


def iota(shape, dim):
    return lax.broadcasted_iota(jnp.int32, shape, dim)


def quarters(x):
    return [x[n * HALF : (n + 1) * HALF] for n in range(4)]


def kernel(
    slabs,
    tiles,
    images,
    mask_in,
    table_in,
    flow_out,
    mesh_out,
    buf,
    mask,
    table,
    z_h,
    z_l,
    spec,
    tops,
    sums,
    outbox,
    inbox,
    plane_sum,
    local_sem,
    img_send,
    img_recv,
    flow_send,
    flow_recv,
    sum_send,
    sum_recv,
):
    z_count = slabs // X_COUNT
    plane = X_COUNT * tiles
    p = lax.axis_index("slab")
    t = lax.axis_index("tile")
    p_next, p_back = lax.rem(p + 1, slabs), lax.rem(p + slabs - 1, slabs)
    t_next, t_back = lax.rem(t + 1, tiles), lax.rem(t + tiles - 1, tiles)
    px, pz = lax.rem(p, X_COUNT), lax.div(p, X_COUNT)
    z_next, z_back = lax.rem(pz + 1, z_count), lax.rem(pz + z_count - 1, z_count)
    at_low, at_high = px == 0, px == X_COUNT - 1

    def in_plane(n):
        x = lax.rem(px + lax.div(n, tiles), X_COUNT)
        return (pz * X_COUNT + x, lax.rem(t + lax.rem(n, tiles), tiles))

    def along_z(n):
        return (lax.rem(pz + n, z_count) * X_COUNT + px, t)

    def signal(device):
        pl.semaphore_signal(barrier, inc=1, device_id=device, device_id_type=MESH)

    own = pltpu.make_async_copy(images, buf.at[pl.ds(1, SEC), pl.ds(RIM, ROWS), :], local_sem.at[0])
    first_tables = pltpu.make_async_copy(table_in.at[pl.ds(0, 4)], table.at[pl.ds(0, 4)], local_sem.at[1])
    other_tables = pltpu.make_async_copy(table_in.at[pl.ds(4, 6)], table.at[pl.ds(4, 6)], local_sem.at[2])
    own_mask = pltpu.make_async_copy(mask_in, mask, local_sem.at[3])
    for copy in (own, first_tables, other_tables, own_mask):
        copy.start()

    barrier = pltpu.get_barrier_semaphore()

    @pl.loop(0, tiles)
    def _(n):
        signal((z_back * X_COUNT + X_COUNT - 1, n))
        signal((z_next * X_COUNT, n))

    @pl.loop(1, plane)
    def _(n):
        signal(in_plane(n))

    @pl.loop(1, z_count)
    def _(n):
        signal(along_z(n))

    def remote(src, dst, send_sem, recv_sem, device):
        return pltpu.make_async_remote_copy(
            src_ref=src,
            dst_ref=dst,
            send_sem=send_sem,
            recv_sem=recv_sem,
            device_id=device,
            device_id_type=MESH,
        )

    top_rim, bottom_rim, middle = pl.ds(0, RIM), pl.ds(RIM + ROWS, RIM), pl.ds(RIM, ROWS)
    first_rows, last_rows = pl.ds(0, RIM), pl.ds(ROWS - RIM, RIM)
    sections, last, below = pl.ds(1, SEC), pl.ds(SEC - 1, 1), pl.ds(0, 1)
    moves = [
        (images.at[last], buf.at[below, middle, :], (p_next, t)),
        (images.at[last, last_rows, :], buf.at[below, top_rim, :], (p_next, t_next)),
        (images.at[last, first_rows, :], buf.at[below, bottom_rim, :], (p_next, t_back)),
        (images.at[:, last_rows, :], buf.at[sections, top_rim, :], (p, t_next)),
        (images.at[:, first_rows, :], buf.at[sections, bottom_rim, :], (p, t_back)),
    ]
    copies = [remote(src, dst, img_send.at[n], img_recv.at[n], device) for n, (src, dst, device) in enumerate(moves)]

    def transform_columns(s, start, count):
        rows = pl.ds(start, count)
        x = split(buf[s, rows, :])
        for n in range(2):
            high, low = split(dot3(x, (table[2 * n], table[2 * n + 1])))
            z_h[s, n, rows, :] = high
            z_l[s, n, rows, :] = low

    def transform_rims(s):
        @pl.when(t == 0)
        def _():
            buf[s, top_rim, :] = jnp.zeros((RIM, COLS), f32)

        @pl.when(t == tiles - 1)
        def _():
            buf[s, bottom_rim, :] = jnp.zeros((RIM, COLS), f32)

        transform_columns(s, 0, RIM)
        transform_columns(s, RIM + ROWS, RIM)

    slot = lax.rem(iota((HALF, COLS), 1), HALF)
    edge = (slot == 0) & (iota((HALF, COLS), 0) > 0)
    corner = (iota((8, COLS), 0) == 0) & (lax.rem(iota((8, COLS), 1), HALF) == 0)
    lag = iota((PATCH, 1), 0)
    lag = jnp.where(lag < PATCH // 2, lag, lag - PATCH).astype(f32)

    def spectrum(s, i):
        rows = pl.ds(pl.multiple_of(i * STRIDE, STRIDE), PATCH)
        stacked = [jnp.concatenate([z[s, 0, rows, :], z[s, 1, rows, :]], axis=0) for z in (z_h, z_l)]
        a, b, c, d = quarters(dot3((table[4], table[5]), stacked))
        spec[s, i, 0:HALF] = jnp.where(edge, a + c, a)
        spec[s, i, HALF : 2 * HALF] = jnp.where(edge, b + d, b)
        spec[s, i, 2 * HALF : 3 * HALF] = jnp.where(edge, b - d, c)
        spec[s, i, 3 * HALF :] = jnp.where(edge, c - a, d)

    def patched(general, special):
        return jnp.concatenate([jnp.where(corner, special, general[:8]), general[8:]], axis=0)

    def pair(earlier, i):
        ap, aq, ar, at = quarters(spec[earlier, i])
        bp, bq, br, bt = quarters(spec[earlier + 1, i])
        xp = patched(ap * bp + aq * bq, 4.0 * ap[:8] * bp[:8])
        xq = patched(ap * bq - aq * bp, 4.0 * aq[:8] * bq[:8])
        xr = patched(ar * br + at * bt, 4.0 * ar[:8] * br[:8])
        xt = patched(ar * bt - at * br, 4.0 * at[:8] * bt[:8])
        cross = jnp.concatenate(
            [
                jnp.where(edge, xp - xt, xp),
                jnp.where(edge, xq + xr, xq),
                jnp.where(edge, xp + xt, xr),
                jnp.where(edge, xq - xr, xt),
            ],
            axis=0,
        )
        u = split(dot3((table[6], table[7]), split(cross)))
        for half in range(2):
            lanes = slice(half * LANES, (half + 1) * LANES)
            stacked = [jnp.concatenate([x[:PATCH, lanes], x[PATCH:, lanes]], axis=1) for x in u]
            scores = dot3(stacked, (table[8], table[9]))
            top = jnp.max(scores, axis=0, keepdims=True)
            weights = jnp.exp2(scores - top)
            total = jnp.sum(weights, axis=0, keepdims=True)
            moment = jnp.sum(weights * lag, axis=0, keepdims=True)
            place = slice(half * COLS, (half + 1) * COLS)
            tops[i, pl.ds(earlier, 1), place] = top
            tops[i, pl.ds(earlier + SEC, 1), place] = top
            sums[i, pl.ds(earlier, 1), place] = total
            sums[i, pl.ds(earlier + SEC, 1), place] = moment

    first_tables.wait()
    own.wait()

    @pl.loop(1, SEC + 1)
    def _(s):
        transform_columns(s, RIM, ROWS)

    pl.semaphore_wait(barrier, plane - 1 + z_count - 1 + plane * jnp.where(at_low | at_high, 1, 0))
    for copy in copies:
        copy.start()
    other_tables.wait()

    @pl.loop(0, 2 * SEC)
    def _(m):
        outer = lax.div(m, SEC)
        step = lax.rem(m, SEC)

        @pl.when(m == SEC)
        def _():
            for copy in copies[3:]:
                copy.wait_recv()

            @pl.loop(1, SEC + 1)
            def _(s):
                transform_rims(s)

        rows = (1 - outer, 2 + outer)
        for i in rows:
            spectrum(step + 1, i)

        @pl.when(step > 0)
        def _():
            for i in rows:
                pair(step, i)

    for copy in copies[:3]:
        copy.wait_recv()
    transform_columns(0, RIM, ROWS)
    transform_rims(0)
    for i in range(NODES):
        spectrum(0, i)
    for i in range(NODES):
        pair(0, i)

    lane8 = iota((8, LANES), 1)
    row8 = iota((8, LANES), 0)
    lag_cols = jnp.where(lane8 < PATCH // 2, lane8, lane8 - PATCH).astype(f32)
    along = jnp.zeros((8, LANES), f32)
    across = jnp.zeros((8, LANES), f32)
    for i in range(NODES):
        for j in range(NODES):
            lanes = slice(j * LANES, (j + 1) * LANES)
            top = tops[i, :, lanes]
            scaled = sums[i, :, lanes] * jnp.exp2(top - jnp.max(top, axis=1, keepdims=True))
            here = lane8 == i * NODES + j
            along = jnp.where(here, jnp.sum(scaled, axis=1, keepdims=True), along)
            across = jnp.where(here, jnp.sum(scaled * lag_cols, axis=1, keepdims=True), across)
    live = lax.rem(row8, SEC) + p > 0
    low_half = row8 < SEC
    numerator = jnp.where(low_half, pltpu.roll(along, SEC, 0), pltpu.roll(across, SEC, 0))
    denominator = jnp.where(low_half, along, pltpu.roll(along, SEC, 0))
    flows = jnp.where(live & (lane8 < BLOCK), numerator / denominator, 0.0)

    own_mask.wait()
    springs = jnp.zeros((8, LANES), f32)
    for i in range(NODES):
        here = jnp.concatenate([mask[s, i : i + 1, :] for s in range(SEC)], axis=0).astype(f32)
        here = jnp.concatenate([here, jnp.zeros((SEC, LANES - NODES), f32)], axis=1)
        here = jnp.concatenate([here, jnp.zeros((SEC, LANES), f32)], axis=0)
        springs = springs + (pltpu.roll(here, i * NODES, 1) if i else here)
    springs = jnp.where(live, springs, 0.0)

    def flat(x):
        return jnp.sum(pltpu.roll(x, 0, 1, stride=BLOCK, stride_axis=0), axis=0, keepdims=True)

    outbox[0:1, :] = flat(flows)
    outbox[1:2, :] = flat(springs)
    inbox[1 + px, t] = outbox[...]

    def to_plane(n):
        return remote(outbox, inbox.at[1 + px, t], flow_send.at[n], flow_recv.at[1 + px, t], in_plane(n))

    def to_next(n):
        return remote(outbox, inbox.at[0, t], flow_send.at[plane + n], flow_recv.at[0, t], (z_next * X_COUNT + lax.div(n, tiles), lax.rem(n, tiles)))

    def to_back(n):
        return remote(outbox, inbox.at[X_COUNT + 1, t], flow_send.at[plane + n], flow_recv.at[X_COUNT + 1, t], (z_back * X_COUNT + lax.div(n, tiles), lax.rem(n, tiles)))

    def from_source(q, n):
        return remote(outbox, inbox.at[q, n], flow_send.at[0], flow_recv.at[q, n], (p_next, t))

    def write(out, x):
        for i in range(NODES):
            moved = pltpu.roll(x, LANES - i * NODES, 1) if i else x
            for c in range(2):
                for s in range(SEC):
                    out[c, s, i : i + 1, :] = moved[c * SEC + s : c * SEC + s + 1, :NODES]


    @pl.when(at_high)
    def _():
        @pl.loop(0, plane)
        def _(n):
            to_next(n).start()

    @pl.when(at_low)
    def _():
        @pl.loop(0, plane)
        def _(n):
            to_back(n).start()

    @pl.loop(1, plane)
    def _(n):
        to_plane(n).start()

    write(flow_out, flows)


    @pl.loop(0, tiles)
    def _(n):
        from_source(0, n).wait_recv()
        from_source(X_COUNT + 1, n).wait_recv()

    @pl.loop(1, plane)
    def _(n):
        x = lax.rem(px + lax.div(n, tiles), X_COUNT)
        from_source(1 + x, lax.rem(t + lax.rem(n, tiles), tiles)).wait_recv()

    block = lax.div(lane8, BLOCK)

    def transpose_blocks(x):
        for bit in (1, 2, 4):
            row_bit, lane_bit = (row8 & bit) > 0, (block & bit) > 0
            up = pltpu.roll(pltpu.roll(x, 8 - bit, 0), BLOCK * bit, 1)
            down = pltpu.roll(pltpu.roll(x, bit, 0), LANES - BLOCK * bit, 1)
            x = jnp.where(row_bit == lane_bit, x, jnp.where(row_bit, down, up))
        return x

    flow_parts, spring_parts = [], []
    for q in range(X_COUNT + 2):
        there = 1.0
        if q == 0:
            there = (pz > 0).astype(f32)
        elif q == X_COUNT + 1:
            there = (pz < z_count - 1).astype(f32)
        flow_q, spring_q = inbox[q, :, 0, :], inbox[q, :, 1, :]
        if tiles < 8:
            pad = jnp.zeros((8 - tiles, LANES), f32)
            flow_q, spring_q = (jnp.concatenate([v, pad], axis=0) for v in (flow_q, spring_q))
        flow_parts.append(there * transpose_blocks(flow_q))
        spring_parts.append(there * transpose_blocks(spring_q)[:SEC])
    wide = (X_COUNT + 2) * SEC
    spring = jnp.concatenate(spring_parts, axis=0)
    flow = [jnp.concatenate([v[c * SEC : (c + 1) * SEC] for v in flow_parts], axis=0) for c in range(2)]
    lane = iota((wide, LANES), 1)
    node_col = lax.rem(lane, NODES)
    live_lanes = (lane < tiles * BLOCK).astype(f32)
    has_up, has_down = (lane >= NODES).astype(f32), (lane < LANES - NODES).astype(f32)
    has_left, has_right = (node_col > 0).astype(f32), (node_col < NODES - 1).astype(f32)

    def differ(stretch):
        return inter_stiff * (pltpu.roll(stretch, wide - 1, 0) - stretch)

    def apply(v):
        stretch = spring * (v - pltpu.roll(v, 1, 0))
        beside = (
            has_up * pltpu.roll(v, NODES, 1)
            + has_down * pltpu.roll(v, LANES - NODES, 1)
            + has_left * pltpu.roll(v, 1, 1)
            + has_right * pltpu.roll(v, LANES - 1, 1)
        )
        return live_lanes * (differ(stretch) + plane_stiff * (beside - 4.0 * v))

    powers = []
    for c in range(2):
        chain = [differ(-spring * flow[c])]
        for _ in range(STEPS - 1):
            chain.append(apply(chain[-1]))
        powers.append(chain)
    grams = [(a, b) for a in range(STEPS) for b in range(a, STEPS)]
    core = slice(SEC, SEC + X_COUNT * SEC)
    rows = [
        jnp.sum(powers[0][a][core] * powers[0][b][core] + powers[1][a][core] * powers[1][b][core], axis=0, keepdims=True)
        for a, b in grams
    ]
    totals = jnp.concatenate(rows + [jnp.zeros((16 - len(grams), LANES), f32)], axis=0)
    totals = jnp.sum(totals, axis=1, keepdims=True)
    diagonal = iota((16, LANES), 0) == iota((16, LANES), 1)
    plane_sum[0:1, :] = jnp.sum(jnp.where(diagonal, totals, 0.0), axis=0, keepdims=True)

    def to_z(n):
        return remote(plane_sum.at[pl.ds(0, 1)], plane_sum.at[pl.ds(n, 1)], sum_send.at[n], sum_recv.at[n], along_z(n))


    @pl.loop(1, z_count)
    def _(n):
        to_z(n).start()

    mine = []
    for a in range(STEPS):
        both = jnp.zeros((8, LANES), f32)
        for q in range(X_COUNT):
            part = slice(SEC + q * SEC, 2 * SEC + q * SEC)
            here = jnp.concatenate([powers[0][a][part], powers[1][a][part]], axis=0)
            both = jnp.where(px == q, here, both)
        mine.append(pltpu.roll(both, lax.rem(LANES - t * BLOCK, LANES), 1))

    for copy in copies:
        copy.wait_send()

    @pl.when(at_low | at_high)
    def _():
        @pl.loop(0, plane)
        def _(n):
            to_next(n).wait_send()

    @pl.loop(1, plane)
    def _(n):
        to_plane(n).wait_send()

    @pl.loop(1, z_count)
    def _(n):
        to_z(n).wait_recv()

    totals = jnp.sum(plane_sum[0:z_count], axis=0, keepdims=True)
    gram = {}
    for n, (a, b) in enumerate(grams):
        gram[a, b] = gram[b, a] = totals[:, n : n + 1]
    count = 2 * SEC * NODES * NODES * slabs * tiles
    zero = jnp.zeros((1, 1), f32)
    force = [zero + 1.0, zero, zero, zero]
    moved = [zero] * STEPS
    for step in range(STEPS):
        square = zero
        for a in range(step + 1):
            square = square + force[a] * force[a] * gram[a, a]
            for b in range(a + 1, step + 1):
                square = square + 2.0 * force[a] * force[b] * gram[a, b]
        scale = step_size / jnp.sqrt(jnp.maximum(square, 0.0) / count + norm_eps)
        moved = [m + scale * f for m, f in zip(moved, force)]
        force = [f + (scale * force[n - 1] if n else 0.0) for n, f in enumerate(force)]
    write(mesh_out, sum(m * v for m, v in zip(moved, mine)))

    @pl.loop(1, z_count)
    def _(n):
        to_z(n).wait_send()


def local(slabs, tiles, images, tissue_mask):
    z_count = max(slabs // X_COUNT, 1)
    plane = X_COUNT * tiles
    vmem = pl.BlockSpec(memory_space=pltpu.VMEM)
    hbm = pl.BlockSpec(memory_space=pltpu.HBM)
    constants = jnp.asarray(tables())
    out = jax.ShapeDtypeStruct((2, SEC, NODES, NODES), f32)
    dma = pltpu.SemaphoreType.DMA
    return pl.pallas_call(
        functools.partial(kernel, slabs, tiles),
        out_shape=(out, out),
        in_specs=[hbm, hbm, hbm],
        out_specs=(vmem, vmem),
        scratch_shapes=[
            pltpu.VMEM((SEC + 1, WIDE, COLS), f32),
            pltpu.VMEM((SEC, NODES, NODES), jnp.int32),
            pltpu.VMEM(constants.shape, bf16),
            pltpu.VMEM((SEC + 1, 2, WIDE, COLS), bf16),
            pltpu.VMEM((SEC + 1, 2, WIDE, COLS), bf16),
            pltpu.VMEM((SEC + 1, NODES, 4 * HALF, COLS), f32),
            pltpu.VMEM((NODES, 2 * SEC, NODES * LANES), f32),
            pltpu.VMEM((NODES, 2 * SEC, NODES * LANES), f32),
            pltpu.VMEM((2, LANES), f32),
            pltpu.VMEM((X_COUNT + 2, tiles, 2, LANES), f32),
            pltpu.VMEM((max(z_count, 8), LANES), f32),
            dma((4,)),
            dma((5,)),
            dma((5,)),
            dma((2 * plane,)),
            dma((X_COUNT + 2, tiles)),
            dma((z_count,)),
            dma((z_count,)),
        ],
        compiler_params=pltpu.CompilerParams(
            collective_id=0, has_side_effects=True, vmem_limit_bytes=64 * 1024 * 1024 - 65536
        ),
    )(images, tissue_mask, constants)


def solution(mesh):
    placed = (P("slab", "tile", None), P("slab", "tile", None))
    return jax.shard_map(
        functools.partial(local, mesh.shape["slab"], mesh.shape["tile"]),
        mesh=mesh,
        in_specs=placed,
        out_specs=(P(None, "slab", "tile", None), P(None, "slab", "tile", None)),
        check_vma=False,
    )
```

time: 66 us -> 50.4 us (0.76)
  the two profiles are of different devices: /device:TPU:2 before, /device:TPU:1 now
where the time goes in v2:
time: 50.4 us; the launch traced here: 50.1 us
  Pallas kernels  46.8 us (93%)
  local copies, waits for them, and re-layouts  2.65 us (5%)
  between operations  0.64 us (1%)
    pallas_call x1, Pallas kernels, local(): pl.pallas_call(functools.partial(kernel, slabs, tiles), out_shape=(out, o...  46.8 us
    unnamed x2, local copies, waits for them, and re-layouts  2.65 us

profile of v2, /device:TPU:1, one launch (start us, length us, event | category | flops | bytes accessed | tf_op | source)
XLA Modules:
  0.0 50.1 jit_solution(8790894739939201533)
XLA Ops:
  0.6 46.8 %shard_map.50 = (f32[2,4,4,4]{3,2,1,0:T(4,128)}, f32[2,4,4,4]{3,2,1,0:T(4,128)}) custom-call(f32[4,256,256]{2,1,0:T(8,128)} %images.1, s32[4,4,4]{2,1,0:T(4,128)} %mask_in.1, bf16[10,256,256]{2,1,0:T(8,128)(2,1)} %constant.2.clone.table_in), custom_call_target="tpu_custom_call" | custom-call | tf_op jit(solution)/shard_map/pallas_call | solution.py:531
  47.5 1.3 %copy.7 = f32[2,4,4,4]{3,2,1,0:T(4,128)} copy(f32[2,4,4,4]{3,2,1,0:T(4,128)} %get-tuple-element.4) | data formatting | bytes 1024
  48.8 1.3 %copy.8 = f32[2,4,4,4]{3,2,1,0:T(4,128)} copy(f32[2,4,4,4]{3,2,1,0:T(4,128)} %get-tuple-element.5) | data formatting | bytes 1024

commit v3 on v2

v3 whole, which is shorter than its diff:
```python
import functools

import jax
import jax.numpy as jnp
import ml_dtypes
import numpy as np
from jax import lax
from jax.experimental import pallas as pl
from jax.experimental.pallas import tpu as pltpu
from jax.sharding import PartitionSpec as P

MESH = pl.DeviceIdType.MESH
PATCH = 128
STRIDE = 64
HALF = 64
RIM = 32
TEMP = 256
STEPS = 4
BLOCK = 16
SPLIT = 160
X_COUNT = 4
COLS = 256
NODES = 4
SEC = 4
ROWS = 256
WIDE = ROWS + 2 * RIM
LANES = 128

inter_stiff = 1.0
plane_stiff = 0.25
step_size = 0.5
norm_eps = 1e-06

f32 = jnp.float32
bf16 = jnp.bfloat16


def pieces(table):
    high = table.astype(np.float32).astype(ml_dtypes.bfloat16)
    low = (table - high.astype(np.float64)).astype(np.float32).astype(ml_dtypes.bfloat16)
    return high, low


def tables():
    k = np.arange(HALF)[:, None]
    x = np.arange(PATCH)[None, :]
    angle = 2.0 * np.pi * ((k * x) % PATCH) / PATCH
    cosine, sine = np.cos(angle), np.sin(angle)
    alternate = np.where(np.arange(PATCH) % 2 == 0, 1.0, -1.0)
    sine[0] = np.where(np.arange(PATCH) % 2 == 0, 1.0, -1.0)
    forward = np.concatenate([cosine, sine], axis=0)
    columns = np.zeros((2, COLS, NODES, HALF))
    for j in range(NODES):
        for y in range(PATCH):
            col = j * STRIDE - RIM + y
            if 0 <= col < COLS:
                columns[0, col, j] = cosine[:, y]
                columns[1, col, j] = sine[:, y]
    columns = columns.reshape(2, COLS, NODES * HALF)
    unit = 2.0 * np.log2(np.e) / (PATCH * PATCH * TEMP)
    final = np.zeros((2, 2, HALF, 2, PATCH))
    for j in range(2):
        final[0, j, :, j] = unit * cosine
        final[1, j, :, j] = unit * sine
    final = final.reshape(4 * HALF, 2 * PATCH)

    def stacked(table):
        high, low = pieces(table)
        return np.block([[high, high], [low, np.zeros_like(low)]])

    return np.stack(
        [stacked(forward), *pieces(columns[0]), *pieces(columns[1]), stacked(forward.T), *pieces(final)]
    )


def split(x):
    high = x.astype(bf16)
    low = (x - high.astype(f32)).astype(bf16)
    return high, low


def dot(a, b):
    return jnp.dot(a, b, preferred_element_type=f32)


def dot3(a, b):
    count = a.shape[0] // 2
    both = dot(a, b[0])
    return both[:count] + both[count:] + dot(a[:count], b[1])


def iota(shape, dim):
    return lax.broadcasted_iota(jnp.int32, shape, dim)


def quarters(x):
    return [x[n * HALF : (n + 1) * HALF] for n in range(4)]


def kernel(
    slabs,
    tiles,
    images,
    mask_in,
    table_in,
    flow_out,
    mesh_out,
    buf,
    mask,
    table,
    x_h,
    x_l,
    y,
    spec,
    first_spec,
    tops,
    sums,
    outbox,
    inbox,
    plane_sum,
    local_sem,
    img_send,
    img_recv,
    flow_send,
    flow_recv,
    sum_send,
    sum_recv,
):
    z_count = max(slabs // X_COUNT, 1)
    plane = X_COUNT * tiles
    p = lax.axis_index("slab")
    t = lax.axis_index("tile")
    p_next, p_back = lax.rem(p + 1, slabs), lax.rem(p + slabs - 1, slabs)
    t_next, t_back = lax.rem(t + 1, tiles), lax.rem(t + tiles - 1, tiles)
    px, pz = lax.rem(p, X_COUNT), lax.div(p, X_COUNT)
    z_next, z_back = lax.rem(pz + 1, z_count), lax.rem(pz + z_count - 1, z_count)
    at_low, at_high = px == 0, px == X_COUNT - 1

    x_ring = [lax.rem(px + a, X_COUNT) for a in range(X_COUNT)]
    t_ring = [lax.rem(t + b, tiles) for b in range(tiles)]
    z_ring = [lax.rem(pz + a, z_count) for a in range(z_count)]

    def hops(step, size):
        return min(step, size - step)

    steps = [(a, b) for a in range(X_COUNT) for b in range(tiles) if a or b]
    steps.sort(key=lambda ab: -hops(ab[0], X_COUNT) - hops(ab[1], tiles) / 2)
    plane_mates = [(pz * X_COUNT + x_ring[a], t_ring[b]) for a, b in steps]
    z_mates = [(z_ring[n] * X_COUNT + px, t) for n in sorted(range(1, z_count), key=lambda n: -hops(n, z_count))]

    def signal(device):
        pl.semaphore_signal(barrier, inc=1, device_id=device, device_id_type=MESH)

    own = pltpu.make_async_copy(images, buf.at[pl.ds(1, SEC), pl.ds(RIM, ROWS), :], local_sem.at[0])
    first_tables = pltpu.make_async_copy(table_in.at[pl.ds(0, 1)], table.at[pl.ds(0, 1)], local_sem.at[1])
    other_tables = pltpu.make_async_copy(table_in.at[pl.ds(1, 7)], table.at[pl.ds(1, 7)], local_sem.at[2])
    own_mask = pltpu.make_async_copy(mask_in, mask, local_sem.at[3])
    for copy in (own, first_tables, other_tables, own_mask):
        copy.start()

    barrier = pltpu.get_barrier_semaphore()

    for device in z_mates:
        signal(device)
    for n in range(tiles):
        signal((z_back * X_COUNT + X_COUNT - 1, n))
        signal((z_next * X_COUNT, n))
    for device in plane_mates:
        signal(device)

    def remote(src, dst, send_sem, recv_sem, device):
        return pltpu.make_async_remote_copy(
            src_ref=src,
            dst_ref=dst,
            send_sem=send_sem,
            recv_sem=recv_sem,
            device_id=device,
            device_id_type=MESH,
        )

    top_rim, bottom_rim = pl.ds(0, RIM), pl.ds(RIM + ROWS, RIM)
    first_rows, last_rows = pl.ds(0, RIM), pl.ds(ROWS - RIM, RIM)
    sections, last, below = pl.ds(1, SEC), pl.ds(SEC - 1, 1), pl.ds(0, 1)
    moves = [
        (images.at[last, pl.ds(0, SPLIT), :], buf.at[below, pl.ds(RIM, SPLIT), :], (p_next, t)),
        (images.at[last, last_rows, :], buf.at[below, top_rim, :], (p_next, t_next)),
        (images.at[last, pl.ds(SPLIT, ROWS - SPLIT), :], buf.at[below, pl.ds(RIM + SPLIT, ROWS - SPLIT), :], (p_next, t)),
        (images.at[last, first_rows, :], buf.at[below, bottom_rim, :], (p_next, t_back)),
        (images.at[:, last_rows, :], buf.at[sections, top_rim, :], (p, t_next)),
        (images.at[:, first_rows, :], buf.at[sections, bottom_rim, :], (p, t_back)),
    ]
    copies = [remote(src, dst, img_send.at[n], img_recv.at[n], device) for n, (src, dst, device) in enumerate(moves)]

    def prepare(s, start, count):
        rows = pl.ds(start, count)
        x_h[s, rows, :], x_l[s, rows, :] = split(buf[s, rows, :])

    def prepare_top(s):
        @pl.when(t == 0)
        def _():
            buf[s, top_rim, :] = jnp.zeros((RIM, COLS), f32)

        prepare(s, 0, RIM)

    def prepare_bottom(s):
        @pl.when(t == tiles - 1)
        def _():
            buf[s, bottom_rim, :] = jnp.zeros((RIM, COLS), f32)

        prepare(s, RIM + ROWS, RIM)

    row_zero = iota((8, COLS), 0) == 0
    lane_zero = lax.rem(iota((8, COLS), 1), HALF) == 0
    corner = row_zero & lane_zero
    lag = iota((PATCH, 1), 0)
    lag = jnp.where(lag < PATCH // 2, lag, lag - PATCH).astype(f32)

    def merged(general, at_lane, at_row):
        lanes = jnp.concatenate([lane_zero] * (HALF // 8), axis=0)
        out = jnp.where(lanes, at_lane, general)
        return jnp.concatenate([jnp.where(row_zero, at_row[:8], out[:8]), out[8:]], axis=0)

    def transform_rows(s, i, place, n):
        rows = pl.ds(pl.multiple_of(i * STRIDE, STRIDE), PATCH)
        window = jnp.concatenate([x_h[s, rows, :], x_l[s, rows, :]], axis=0)
        both = dot(table[0], window)
        high, low = split(both[:PATCH] + both[PATCH:])
        y[place, n * PATCH : (n + 1) * PATCH] = high
        y[place, (2 + n) * PATCH : (3 + n) * PATCH] = low

    def spectra(place):
        rows = y[place]
        c = dot3(rows, (table[1], table[2]))
        d = dot3(rows, (table[3], table[4]))
        found = []
        for n in range(2):
            cc, sc = c[2 * n * HALF : (2 * n + 1) * HALF], c[(2 * n + 1) * HALF : (2 * n + 2) * HALF]
            cs, ss = d[2 * n * HALF : (2 * n + 1) * HALF], d[(2 * n + 1) * HALF : (2 * n + 2) * HALF]
            found.append(
                [
                    merged(cc - ss, cc, cc),
                    merged(cs + sc, sc, cs),
                    merged(cc + ss, cs, sc),
                    merged(sc - cs, ss, ss),
                ]
            )
        return found

    def keep(ref, index, parts):
        for n, part in enumerate(parts):
            ref[index, n * HALF : (n + 1) * HALF] = part

    def patched(general, special):
        return jnp.concatenate([jnp.where(corner, special, general[:8]), general[8:]], axis=0)

    def correlate(first, second):
        ap, aq, ar, at = quarters(first)
        bp, bq, br, bt = quarters(second)
        xp = patched(ap * bp + aq * bq, 0.5 * ap[:8] * bp[:8])
        xq = patched(ap * bq - aq * bp, 0.5 * aq[:8] * bq[:8])
        xr = patched(ar * br + at * bt, 0.5 * ar[:8] * br[:8])
        xt = patched(ar * bt - at * br, 0.5 * at[:8] * bt[:8])
        cosines = split(jnp.concatenate([merged(xp + xr, xp, xp), merged(xq + xt, xq, xr)], axis=0))
        sines = split(jnp.concatenate([merged(xq - xt, xr, xq), merged(xr - xp, xt, xt)], axis=0))
        parts = []
        for v in (cosines, sines):
            both = dot(table[5], jnp.concatenate(v, axis=0))
            parts.append(split(both[:PATCH] + both[PATCH:]))
        (c_h, c_l), (s_h, s_l) = parts
        lanes = [slice(n * LANES, (n + 1) * LANES) for n in range(2)]
        high = [jnp.concatenate([c_h[:, k], s_h[:, k]], axis=1) for k in lanes]
        low = [jnp.concatenate([c_l[:, k], s_l[:, k]], axis=1) for k in lanes]
        return high, low

    def pairs(earlier, rows, firsts, seconds):
        high, low = [], []
        for first, second in zip(firsts, seconds):
            more_high, more_low = correlate(first, second)
            high += more_high
            low += more_low
        both = dot3(jnp.concatenate(high + low, axis=0), (table[6], table[7]))
        for n in range(2 * len(rows)):
            i, half = rows[n // 2], n % 2
            scores = both[n * PATCH : (n + 1) * PATCH]
            top = jnp.max(scores, axis=0, keepdims=True)
            weights = jnp.exp2(scores - top)
            total = jnp.sum(weights, axis=0, keepdims=True)
            moment = jnp.sum(weights * lag, axis=0, keepdims=True)
            place = slice(half * COLS, (half + 1) * COLS)
            tops[i, pl.ds(earlier, 1), place] = top
            tops[i, pl.ds(earlier + SEC, 1), place] = top
            sums[i, pl.ds(earlier, 1), place] = total
            sums[i, pl.ds(earlier + SEC, 1), place] = moment

    def begin():
        pl.semaphore_wait(barrier, plane - 1 + z_count - 1 + plane * jnp.where(at_low | at_high, 1, 0))
        for copy in copies:
            copy.start()

    own.wait()
    for s in range(1, SEC + 1):
        prepare(s, RIM, ROWS)
    first_tables.wait()
    for s in range(1, SEC + 1):
        for n in range(2):
            transform_rows(s, 1 + n, s, n)
    begin()
    other_tables.wait()

    @pl.loop(0, 2)
    def _(outer):
        rows = (1 - outer, 2 + outer)

        @pl.when(outer == 1)
        def _():
            for copy in copies[4:]:
                copy.wait_recv()
            for s in range(1, SEC + 1):
                prepare_top(s)
                prepare_bottom(s)
            for s in range(1, SEC + 1):
                for n in range(2):
                    transform_rows(s, 3 * n, s, n)

        for s in range(1, SEC + 1):
            for n, parts in enumerate(spectra(s)):
                if s == 1:
                    keep(first_spec, rows[n], parts)
                keep(spec, (s - 1) * 2 + n, parts)
            if s > 1:
                pairs(s - 1, rows, [spec[(s - 2) * 2 + n] for n in range(2)], [spec[(s - 1) * 2 + n] for n in range(2)])

    for n in range(2):
        for copy in copies[2 * n : 2 * n + 2]:
            copy.wait_recv()
        if n == 0:
            prepare_top(0)
            prepare(0, RIM, SPLIT)
        else:
            prepare(0, RIM + SPLIT, ROWS - SPLIT)
            prepare_bottom(0)
        rows = (2 * n, 2 * n + 1)
        for k in range(2):
            transform_rows(0, rows[k], n, k)
        for k, parts in enumerate(spectra(n)):
            keep(spec, rows[k], parts)
        pairs(0, rows, [spec[i] for i in rows], [first_spec[i] for i in rows])

    lane8 = iota((8, LANES), 1)
    row8 = iota((8, LANES), 0)
    lag_cols = jnp.where(lane8 < PATCH // 2, lane8, lane8 - PATCH).astype(f32)
    along = jnp.zeros((8, LANES), f32)
    across = jnp.zeros((8, LANES), f32)
    for i in range(NODES):
        for j in range(NODES):
            lanes = slice(j * LANES, (j + 1) * LANES)
            top = tops[i, :, lanes]
            scaled = sums[i, :, lanes] * jnp.exp2(top - jnp.max(top, axis=1, keepdims=True))
            here = lane8 == i * NODES + j
            along = jnp.where(here, jnp.sum(scaled, axis=1, keepdims=True), along)
            across = jnp.where(here, jnp.sum(scaled * lag_cols, axis=1, keepdims=True), across)
    live = lax.rem(row8, SEC) + p > 0
    low_half = row8 < SEC
    numerator = jnp.where(low_half, pltpu.roll(along, SEC, 0), pltpu.roll(across, SEC, 0))
    denominator = jnp.where(low_half, along, pltpu.roll(along, SEC, 0))
    flows = jnp.where(live & (lane8 < BLOCK), numerator / denominator, 0.0)

    own_mask.wait()
    springs = jnp.zeros((8, LANES), f32)
    for i in range(NODES):
        here = jnp.concatenate([mask[s, i : i + 1, :] for s in range(SEC)], axis=0).astype(f32)
        here = jnp.concatenate([here, jnp.zeros((SEC, LANES - NODES), f32)], axis=1)
        here = jnp.concatenate([here, jnp.zeros((SEC, LANES), f32)], axis=0)
        springs = springs + (pltpu.roll(here, i * NODES, 1) if i else here)
    springs = jnp.where(live, springs, 0.0)

    def flat(x):
        return jnp.sum(pltpu.roll(x, 0, 1, stride=BLOCK, stride_axis=0), axis=0, keepdims=True)

    outbox[0, 0:1, :] = flat(flows)
    outbox[0, 1:2, :] = flat(springs)
    inbox[(1 + px) * tiles + t] = outbox[0]

    def give(q, sem, device):
        return remote(outbox, inbox.at[pl.ds(q * tiles + t, 1)], flow_send.at[sem], flow_recv, device)

    def whole(ref, count, sem):
        slots = ref.at[pl.ds(0, count)]
        pltpu.make_async_copy(slots, slots, sem).wait()

    def write(out, x):
        for i in range(NODES):
            moved = pltpu.roll(x, LANES - i * NODES, 1) if i else x
            for c in range(2):
                for s in range(SEC):
                    out[c, s, i : i + 1, :] = moved[c * SEC + s : c * SEC + s + 1, :NODES]

    @pl.when(at_high)
    def _():
        for x in range(X_COUNT):
            for n in range(tiles):
                give(0, 1, (z_next * X_COUNT + x, n)).start()

    @pl.when(at_low)
    def _():
        for x in range(X_COUNT):
            for n in range(tiles):
                give(X_COUNT + 1, 1, (z_back * X_COUNT + x, n)).start()

    for device in plane_mates:
        give(1 + px, 0, device).start()

    write(flow_out, flows)

    whole(inbox, plane - 1 + 2 * tiles, flow_recv)

    block = lax.div(lane8, BLOCK)

    def transpose_blocks(x):
        for bit in (1, 2, 4):
            row_bit, lane_bit = (row8 & bit) > 0, (block & bit) > 0
            up = pltpu.roll(pltpu.roll(x, 8 - bit, 0), BLOCK * bit, 1)
            down = pltpu.roll(pltpu.roll(x, bit, 0), LANES - BLOCK * bit, 1)
            x = jnp.where(row_bit == lane_bit, x, jnp.where(row_bit, down, up))
        return x

    flow_parts, spring_parts = [], []
    for q in range(X_COUNT + 2):
        there = 1.0
        if q == 0:
            there = (pz > 0).astype(f32)
        elif q == X_COUNT + 1:
            there = (pz < z_count - 1).astype(f32)
        here = slice(q * tiles, (q + 1) * tiles)
        flow_q, spring_q = inbox[here, 0, :], inbox[here, 1, :]
        if tiles < 8:
            pad = jnp.zeros((8 - tiles, LANES), f32)
            flow_q, spring_q = (jnp.concatenate([v, pad], axis=0) for v in (flow_q, spring_q))
        flow_parts.append(there * transpose_blocks(flow_q))
        spring_parts.append(there * transpose_blocks(spring_q)[:SEC])
    wide = (X_COUNT + 2) * SEC
    spring = jnp.concatenate(spring_parts, axis=0)
    flow = [jnp.concatenate([v[c * SEC : (c + 1) * SEC] for v in flow_parts], axis=0) for c in range(2)]
    lane = iota((wide, LANES), 1)
    node_col = lax.rem(lane, NODES)
    live_lanes = (lane < tiles * BLOCK).astype(f32)
    has_up, has_down = (lane >= NODES).astype(f32), (lane < LANES - NODES).astype(f32)
    has_left, has_right = (node_col > 0).astype(f32), (node_col < NODES - 1).astype(f32)

    def differ(stretch):
        return inter_stiff * (pltpu.roll(stretch, wide - 1, 0) - stretch)

    def apply(v):
        stretch = spring * (v - pltpu.roll(v, 1, 0))
        beside = (
            has_up * pltpu.roll(v, NODES, 1)
            + has_down * pltpu.roll(v, LANES - NODES, 1)
            + has_left * pltpu.roll(v, 1, 1)
            + has_right * pltpu.roll(v, LANES - 1, 1)
        )
        return live_lanes * (differ(stretch) + plane_stiff * (beside - 4.0 * v))

    powers = []
    for c in range(2):
        chain = [differ(-spring * flow[c])]
        for _ in range(STEPS - 1):
            chain.append(apply(chain[-1]))
        powers.append(chain)
    grams = [(a, b) for a in range(STEPS) for b in range(a, STEPS)]
    core = slice(SEC, SEC + X_COUNT * SEC)
    rows = [
        jnp.sum(powers[0][a][core] * powers[0][b][core] + powers[1][a][core] * powers[1][b][core], axis=0, keepdims=True)
        for a, b in grams
    ]
    totals = jnp.concatenate(rows + [jnp.zeros((16 - len(grams), LANES), f32)], axis=0)
    totals = jnp.sum(totals, axis=1, keepdims=True)
    diagonal = iota((16, LANES), 0) == iota((16, LANES), 1)
    plane_sum[0] = jnp.sum(jnp.where(diagonal, totals, 0.0), axis=0, keepdims=True)

    def to_z(n):
        slot = pl.ds(n, 1)
        return remote(plane_sum.at[pl.ds(0, 1)], plane_sum.at[slot], sum_send, sum_recv, z_by_step[n])

    z_by_step = [(z_ring[n] * X_COUNT + px, t) for n in range(z_count)]
    for n in sorted(range(1, z_count), key=lambda n: -hops(n, z_count)):
        to_z(n).start()

    mine = []
    for a in range(STEPS):
        both = jnp.zeros((8, LANES), f32)
        for q in range(X_COUNT):
            part = slice(SEC + q * SEC, 2 * SEC + q * SEC)
            here = jnp.concatenate([powers[0][a][part], powers[1][a][part]], axis=0)
            both = jnp.where(px == q, here, both)
        mine.append(pltpu.roll(both, lax.rem(LANES - t * BLOCK, LANES), 1))

    for copy in copies:
        copy.wait_send()

    whole(inbox, plane - 1, flow_send.at[0])

    @pl.when(at_low | at_high)
    def _():
        whole(inbox, plane, flow_send.at[1])

    whole(plane_sum, z_count - 1, sum_recv)

    totals = jnp.sum(plane_sum[0:z_count, 0, :], axis=0, keepdims=True)
    gram = {}
    for n, (a, b) in enumerate(grams):
        gram[a, b] = gram[b, a] = totals[:, n : n + 1]
    count = 2 * SEC * NODES * NODES * slabs * tiles
    zero = jnp.zeros((1, 1), f32)
    force = [zero + 1.0, zero, zero, zero]
    moved = [zero] * STEPS
    for step in range(STEPS):
        square = zero
        for a in range(step + 1):
            square = square + force[a] * force[a] * gram[a, a]
            for b in range(a + 1, step + 1):
                square = square + 2.0 * force[a] * force[b] * gram[a, b]
        scale = step_size / jnp.sqrt(jnp.maximum(square, 0.0) / count + norm_eps)
        moved = [m + scale * f for m, f in zip(moved, force)]
        force = [f + (scale * force[n - 1] if n else 0.0) for n, f in enumerate(force)]
    write(mesh_out, sum(m * v for m, v in zip(moved, mine)))
    whole(plane_sum, z_count - 1, sum_send)


def local(slabs, tiles, images, tissue_mask):
    z_count = max(slabs // X_COUNT, 1)
    plane = X_COUNT * tiles
    vmem = pl.BlockSpec(memory_space=pltpu.VMEM)
    hbm = pl.BlockSpec(memory_space=pltpu.HBM)
    constants = jnp.asarray(tables())
    out = jax.ShapeDtypeStruct((2, SEC, NODES, NODES), f32)
    dma = pltpu.SemaphoreType.DMA
    return pl.pallas_call(
        functools.partial(kernel, slabs, tiles),
        out_shape=(out, out),
        in_specs=[hbm, hbm, hbm],
        out_specs=(vmem, vmem),
        scratch_shapes=[
            pltpu.VMEM((SEC + 1, WIDE, COLS), f32),
            pltpu.VMEM((SEC, NODES, NODES), jnp.int32),
            pltpu.VMEM(constants.shape, bf16),
            pltpu.VMEM((SEC + 1, WIDE, COLS), bf16),
            pltpu.VMEM((SEC + 1, WIDE, COLS), bf16),
            pltpu.VMEM((SEC + 1, 4 * PATCH, COLS), bf16),
            pltpu.VMEM((2 * SEC, 4 * HALF, COLS), f32),
            pltpu.VMEM((NODES, 4 * HALF, COLS), f32),
            pltpu.VMEM((NODES, 2 * SEC, NODES * LANES), f32),
            pltpu.VMEM((NODES, 2 * SEC, NODES * LANES), f32),
            pltpu.VMEM((1, 2, LANES), f32),
            pltpu.VMEM(((X_COUNT + 2) * tiles, 2, LANES), f32),
            pltpu.VMEM((z_count, 1, LANES), f32),
            dma((4,)),
            dma((6,)),
            dma((6,)),
            dma((2,)),
            dma,
            dma,
            dma,
        ],
        compiler_params=pltpu.CompilerParams(
            collective_id=0, has_side_effects=True, vmem_limit_bytes=64 * 1024 * 1024 - 65536
        ),
    )(images, tissue_mask, constants)


def solution(mesh):
    placed = (P("slab", "tile", None), P("slab", "tile", None))
    return jax.shard_map(
        functools.partial(local, mesh.shape["slab"], mesh.shape["tile"]),
        mesh=mesh,
        in_specs=placed,
        out_specs=(P(None, "slab", "tile", None), P(None, "slab", "tile", None)),
        check_vma=False,
    )
```

time: 50.4 us -> 44.6 us (0.88)
  Pallas kernels: 46.8 us -> 41.8 us
  local copies, waits for them, and re-layouts: 2.65 us -> 1.94 us
    pallas_call x1, Pallas kernels: 46.8 us -> 41.8 us  [local(): pl.pallas_call(functools.partial(kernel, slabs, tiles), out_shape=(out, o...]
    unnamed x2 -> x4, local copies, waits for them, and re-layouts: 2.65 us -> 1.94 us
where the time goes in v3:
time: 44.6 us; the launch traced here: 44.4 us
  Pallas kernels  41.8 us (94%)
  local copies, waits for them, and re-layouts  1.94 us (4%)
  between operations  0.65 us (1%)
    pallas_call x1, Pallas kernels, local(): pl.pallas_call(functools.partial(kernel, slabs, tiles), out_shape=(out, o...  41.8 us
    unnamed x4, local copies, waits for them, and re-layouts  1.94 us

profile of v3, /device:TPU:1, one launch (start us, length us, event | category | flops | bytes accessed | tf_op | source)
XLA Modules:
  0.0 44.4 jit_solution(13973699688801150839)
XLA Ops:
  0.6 41.8 %shard_map.50 = (f32[2,4,4,4]{3,2,1,0:T(4,128)}, f32[2,4,4,4]{3,2,1,0:T(4,128)}) custom-call(f32[4,256,256]{2,1,0:T(8,128)} %images.1, s32[4,4,4]{2,1,0:T(4,128)} %mask_in.1, bf16[8,256,256]{2,1,0:T(8,128)(2,1)} %constant.2.clone.table_in), custom_call_target="tpu_custom_call" | custom-call | tf_op jit(solution)/shard_map/pallas_call | solution.py:537
  42.4 0.0 copy-start
  42.5 1.3 %copy.7 = f32[2,4,4,4]{3,2,1,0:T(4,128)} copy(f32[2,4,4,4]{3,2,1,0:T(4,128)} %get-tuple-element.4) | data formatting | bytes 1024
  43.8 0.0 copy-done
  43.8 0.6 %copy.8 = f32[2,4,4,4]{3,2,1,0:T(4,128)} copy(f32[2,4,4,4]{3,2,1,0:T(4,128)S(1)} %copy-done) | data formatting | bytes 1024
Async XLA Ops:
  42.4 1.3 %copy-start = (f32[2,4,4,4]{3,2,1,0:T(4,128)S(1)}, f32[2,4,4,4]{3,2,1,0:T(4,128)}, u32[]{:S(2)}) copy-start(f32[2,4,4,4]{3,2,1,0:T(4,128)} %get-tuple-element.5) | copy-start | bytes 1540

commit v4 on v3

--- a/solution.py
+++ b/solution.py
@@ -49,28 +49,19 @@
     alternate = np.where(np.arange(PATCH) % 2 == 0, 1.0, -1.0)
     sine[0] = np.where(np.arange(PATCH) % 2 == 0, 1.0, -1.0)
     forward = np.concatenate([cosine, sine], axis=0)
-    columns = np.zeros((2, COLS, NODES, HALF))
-    for j in range(NODES):
-        for y in range(PATCH):
-            col = j * STRIDE - RIM + y
-            if 0 <= col < COLS:
-                columns[0, col, j] = cosine[:, y]
-                columns[1, col, j] = sine[:, y]
-    columns = columns.reshape(2, COLS, NODES * HALF)
-    unit = 2.0 * np.log2(np.e) / (PATCH * PATCH * TEMP)
-    final = np.zeros((2, 2, HALF, 2, PATCH))
-    for j in range(2):
-        final[0, j, :, j] = unit * cosine
-        final[1, j, :, j] = unit * sine
-    final = final.reshape(4 * HALF, 2 * PATCH)
-
-    def stacked(table):
+    back = forward.T
+    final = forward * (2.0 * np.log2(np.e) / (PATCH * PATCH * TEMP))
+
+    def from_left(table):
         high, low = pieces(table)
         return np.block([[high, high], [low, np.zeros_like(low)]])
 
-    return np.stack(
-        [stacked(forward), *pieces(columns[0]), *pieces(columns[1]), stacked(forward.T), *pieces(final)]
-    )
+    def from_right(table):
+        high, low = pieces(table)
+        return np.block([[high, low], [high, np.zeros_like(low)]])
+
+    even, odd = np.roll(back, -RIM, axis=0), np.roll(back, RIM, axis=0)
+    return np.stack([from_left(forward), from_right(even), from_right(odd), from_left(back), from_right(final)])
 
 
 def split(x):
@@ -83,18 +74,8 @@
     return jnp.dot(a, b, preferred_element_type=f32)
 
 
-def dot3(a, b):
-    count = a.shape[0] // 2
-    both = dot(a, b[0])
-    return both[:count] + both[count:] + dot(a[:count], b[1])
-
-
 def iota(shape, dim):
     return lax.broadcasted_iota(jnp.int32, shape, dim)
-
-
-def quarters(x):
-    return [x[n * HALF : (n + 1) * HALF] for n in range(4)]
 
 
 def kernel(
@@ -125,6 +106,7 @@
     flow_recv,
     sum_send,
     sum_recv,
+    relay,
 ):
     z_count = max(slabs // X_COUNT, 1)
     plane = X_COUNT * tiles
@@ -146,21 +128,34 @@
     steps = [(a, b) for a in range(X_COUNT) for b in range(tiles) if a or b]
     steps.sort(key=lambda ab: -hops(ab[0], X_COUNT) - hops(ab[1], tiles) / 2)
     plane_mates = [(pz * X_COUNT + x_ring[a], t_ring[b]) for a, b in steps]
-    z_mates = [(z_ring[n] * X_COUNT + px, t) for n in sorted(range(1, z_count), key=lambda n: -hops(n, z_count))]
+    z_by_step = [(z_ring[n] * X_COUNT + px, t) for n in range(z_count)]
+    near_z = [z_by_step[1 % z_count], z_by_step[z_count - 1]]
+    reaches = []
+    while 2 ** len(reaches) < z_count // 2:
+        reaches.append(2 ** len(reaches))
+
+    def tell(n):
+        if n < len(reaches):
+            for step in (reaches[n], z_count - reaches[n]):
+                pl.semaphore_signal(relay.at[n], inc=1, device_id=z_by_step[step], device_id_type=MESH)
+
+    def hear(n):
+        if n < len(reaches):
+            pl.semaphore_wait(relay.at[n], 2)
 
     def signal(device):
         pl.semaphore_signal(barrier, inc=1, device_id=device, device_id_type=MESH)
 
     own = pltpu.make_async_copy(images, buf.at[pl.ds(1, SEC), pl.ds(RIM, ROWS), :], local_sem.at[0])
     first_tables = pltpu.make_async_copy(table_in.at[pl.ds(0, 1)], table.at[pl.ds(0, 1)], local_sem.at[1])
-    other_tables = pltpu.make_async_copy(table_in.at[pl.ds(1, 7)], table.at[pl.ds(1, 7)], local_sem.at[2])
+    other_tables = pltpu.make_async_copy(table_in.at[pl.ds(1, 4)], table.at[pl.ds(1, 4)], local_sem.at[2])
     own_mask = pltpu.make_async_copy(mask_in, mask, local_sem.at[3])
     for copy in (own, first_tables, other_tables, own_mask):
         copy.start()
 
     barrier = pltpu.get_barrier_semaphore()
 
-    for device in z_mates:
+    for device in near_z:
         signal(device)
     for n in range(tiles):
         signal((z_back * X_COUNT + X_COUNT - 1, n))
@@ -209,93 +204,123 @@
 
         prepare(s, RIM + ROWS, RIM)
 
-    row_zero = iota((8, COLS), 0) == 0
-    lane_zero = lax.rem(iota((8, COLS), 1), HALF) == 0
-    corner = row_zero & lane_zero
+    lane_row = iota((1, LANES), 1)
+    left = lane_row < HALF
+    special = (lane_row == 0, lane_row == HALF)
+
+    def by_lane(first, second, at_first, at_second):
+        value = jnp.where(left, first, second)
+        value = jnp.where(special[0], at_first, value)
+        return jnp.where(special[1], at_second, value).astype(f32)
+
+    def turn(x):
+        return pltpu.roll(x, HALF, 1)
+
+    left_plus = jnp.where(left, 1.0, -1.0).astype(f32)
+    to_x = (by_lane(1.0, 1.0, 1.0, 0.0), by_lane(-1.0, 1.0, 0.0, 1.0))
+    to_y = (by_lane(1.0, 1.0, 0.0, 1.0), by_lane(1.0, -1.0, 1.0, 0.0))
+    to_x_turned, to_y_turned = ([turn(v) for v in pair] for pair in (to_x, to_y))
+    to_m = (by_lane(1.0, 1.0, 0.0, 1.0), by_lane(-1.0, -1.0, 1.0, 0.0))
+    to_c = (by_lane(1.0, 1.0, 1.0, 0.0), by_lane(1.0, 1.0, 0.0, 0.0), by_lane(0.0, 0.0, 0.0, 1.0))
+    to_s = (by_lane(1.0, -1.0, 1.0, 0.0), by_lane(0.0, 0.0, 0.0, -1.0))
+    row_zero = iota((8, LANES), 0) == 0
+    corner = row_zero & (lax.rem(iota((8, LANES), 1), HALF) == 0)
+    lane_tall = iota((PATCH, LANES), 1)
+    left_tall = lane_tall < HALF
     lag = iota((PATCH, 1), 0)
     lag = jnp.where(lag < PATCH // 2, lag, lag - PATCH).astype(f32)
 
-    def merged(general, at_lane, at_row):
-        lanes = jnp.concatenate([lane_zero] * (HALF // 8), axis=0)
-        out = jnp.where(lanes, at_lane, general)
-        return jnp.concatenate([jnp.where(row_zero, at_row[:8], out[:8]), out[8:]], axis=0)
+    def at_row_zero(value, general):
+        return jnp.concatenate([jnp.where(row_zero, value[:8], general[:8]), general[8:]], axis=0)
+
+    def windows(v):
+        first, second = v[:, :LANES], v[:, LANES:]
+        return [
+            jnp.where(lane_tall < LANES - RIM, first, 0.0),
+            jnp.where(lane_tall < RIM, second, first),
+            jnp.where(lane_tall < LANES - RIM, second, first),
+            jnp.where(lane_tall < RIM, 0.0, second),
+        ]
 
     def transform_rows(s, i, place, n):
         rows = pl.ds(pl.multiple_of(i * STRIDE, STRIDE), PATCH)
         window = jnp.concatenate([x_h[s, rows, :], x_l[s, rows, :]], axis=0)
         both = dot(table[0], window)
-        high, low = split(both[:PATCH] + both[PATCH:])
-        y[place, n * PATCH : (n + 1) * PATCH] = high
-        y[place, (2 + n) * PATCH : (3 + n) * PATCH] = low
+        for j, part in enumerate(windows(both[:PATCH] + both[PATCH:])):
+            start = (n * 2 + j // 2) * PATCH
+            y[place, j % 2, start : start + PATCH] = jnp.concatenate(split(part), axis=1)
 
     def spectra(place):
-        rows = y[place]
-        c = dot3(rows, (table[1], table[2]))
-        d = dot3(rows, (table[3], table[4]))
+        both = [dot(y[place, k], table[1 + k]) for k in range(2)]
+        both = [x[:, :LANES] + x[:, LANES:] for x in both]
         found = []
         for n in range(2):
-            cc, sc = c[2 * n * HALF : (2 * n + 1) * HALF], c[(2 * n + 1) * HALF : (2 * n + 2) * HALF]
-            cs, ss = d[2 * n * HALF : (2 * n + 1) * HALF], d[(2 * n + 1) * HALF : (2 * n + 2) * HALF]
-            found.append(
-                [
-                    merged(cc - ss, cc, cc),
-                    merged(cs + sc, sc, cs),
-                    merged(cc + ss, cs, sc),
-                    merged(sc - cs, ss, ss),
-                ]
-            )
+            plain, turned = [], []
+            for j in range(NODES):
+                start = (n * 2 + j // 2) * PATCH
+                c, d = both[j % 2][start : start + HALF], both[j % 2][start + HALF : start + PATCH]
+                c_turned, d_turned = turn(c), turn(d)
+                x_part = at_row_zero(c, c * to_x[0] + d_turned * to_x[1])
+                y_part = at_row_zero(d * left_plus, c * to_y[0] + d_turned * to_y[1])
+                plain.append(jnp.concatenate([x_part, y_part], axis=0))
+                x_part = at_row_zero(c_turned, c_turned * to_x_turned[0] + d * to_x_turned[1])
+                y_part = at_row_zero(-d_turned * left_plus, c_turned * to_y_turned[0] + d * to_y_turned[1])
+                turned.append(jnp.concatenate([x_part, y_part], axis=0))
+            found.append((plain, turned))
         return found
 
-    def keep(ref, index, parts):
-        for n, part in enumerate(parts):
-            ref[index, n * HALF : (n + 1) * HALF] = part
-
-    def patched(general, special):
-        return jnp.concatenate([jnp.where(corner, special, general[:8]), general[8:]], axis=0)
+    def keep(ref, index, found):
+        for n, parts in enumerate(found):
+            for j, part in enumerate(parts):
+                ref[index, n, j] = part
+
+    def cross(first, second, j):
+        a, a_turned = first[0, j], first[1, j]
+        b, b_turned = second[0, j], second[1, j]
+        whole = jnp.where(left_tall, a, a_turned) * b + jnp.where(left_tall, a_turned, -a) * b_turned
+        alone = 0.5 * a * b
+        x = jnp.concatenate([jnp.where(corner, alone[:8], whole[:8]), whole[8:HALF]], axis=0)
+        low = whole[HALF:]
+        z = jnp.concatenate([jnp.where(corner, alone[HALF : HALF + 8] * left_plus, low[:8]), low[8:]], axis=0)
+        m = turn(x * to_m[0] + z * to_m[1])
+        cosines = at_row_zero(x, x * to_c[0] + z * to_c[1] + m * to_c[2])
+        sines = at_row_zero(z * left_plus, m * to_s[0] + z * to_s[1])
+        return split(jnp.concatenate([cosines, sines], axis=0))
 
     def correlate(first, second):
-        ap, aq, ar, at = quarters(first)
-        bp, bq, br, bt = quarters(second)
-        xp = patched(ap * bp + aq * bq, 0.5 * ap[:8] * bp[:8])
-        xq = patched(ap * bq - aq * bp, 0.5 * aq[:8] * bq[:8])
-        xr = patched(ar * br + at * bt, 0.5 * ar[:8] * br[:8])
-        xt = patched(ar * bt - at * br, 0.5 * at[:8] * bt[:8])
-        cosines = split(jnp.concatenate([merged(xp + xr, xp, xp), merged(xq + xt, xq, xr)], axis=0))
-        sines = split(jnp.concatenate([merged(xq - xt, xr, xq), merged(xr - xp, xt, xt)], axis=0))
-        parts = []
-        for v in (cosines, sines):
-            both = dot(table[5], jnp.concatenate(v, axis=0))
-            parts.append(split(both[:PATCH] + both[PATCH:]))
-        (c_h, c_l), (s_h, s_l) = parts
-        lanes = [slice(n * LANES, (n + 1) * LANES) for n in range(2)]
-        high = [jnp.concatenate([c_h[:, k], s_h[:, k]], axis=1) for k in lanes]
-        low = [jnp.concatenate([c_l[:, k], s_l[:, k]], axis=1) for k in lanes]
-        return high, low
+        out = []
+        for j in range(0, NODES, 2):
+            parts = [cross(first, second, j + k) for k in range(2)]
+            window = jnp.concatenate([jnp.concatenate([part[h] for part in parts], axis=1) for h in range(2)], axis=0)
+            both = dot(table[3], window)
+            high, low = split(both[:PATCH] + both[PATCH:])
+            for k in range(2):
+                lanes = slice(k * LANES, (k + 1) * LANES)
+                out.append(jnp.concatenate([high[:, lanes], low[:, lanes]], axis=1))
+        return out
 
     def pairs(earlier, rows, firsts, seconds):
-        high, low = [], []
-        for first, second in zip(firsts, seconds):
-            more_high, more_low = correlate(first, second)
-            high += more_high
-            low += more_low
-        both = dot3(jnp.concatenate(high + low, axis=0), (table[6], table[7]))
-        for n in range(2 * len(rows)):
-            i, half = rows[n // 2], n % 2
+        parts = [part for first, second in zip(firsts, seconds) for part in correlate(first, second)]
+        both = dot(jnp.concatenate(parts, axis=0), table[4])
+        both = both[:, :LANES] + both[:, LANES:]
+        for n in range(NODES * len(rows)):
+            i, j = rows[n // NODES], n % NODES
             scores = both[n * PATCH : (n + 1) * PATCH]
             top = jnp.max(scores, axis=0, keepdims=True)
             weights = jnp.exp2(scores - top)
             total = jnp.sum(weights, axis=0, keepdims=True)
             moment = jnp.sum(weights * lag, axis=0, keepdims=True)
-            place = slice(half * COLS, (half + 1) * COLS)
+            place = slice(j * LANES, (j + 1) * LANES)
             tops[i, pl.ds(earlier, 1), place] = top
             tops[i, pl.ds(earlier + SEC, 1), place] = top
             sums[i, pl.ds(earlier, 1), place] = total
             sums[i, pl.ds(earlier + SEC, 1), place] = moment
 
     def begin():
-        pl.semaphore_wait(barrier, plane - 1 + z_count - 1 + plane * jnp.where(at_low | at_high, 1, 0))
+        pl.semaphore_wait(barrier, plane - 1 + 2 + plane * jnp.where(at_low | at_high, 1, 0))
         for copy in copies:
             copy.start()
+        tell(0)
 
     own.wait()
     for s in range(1, SEC + 1):
@@ -313,6 +338,8 @@
 
         @pl.when(outer == 1)
         def _():
+            hear(0)
+            tell(1)
             for copy in copies[4:]:
                 copy.wait_recv()
             for s in range(1, SEC + 1):
@@ -328,8 +355,10 @@
                     keep(first_spec, rows[n], parts)
                 keep(spec, (s - 1) * 2 + n, parts)
             if s > 1:
-                pairs(s - 1, rows, [spec[(s - 2) * 2 + n] for n in range(2)], [spec[(s - 1) * 2 + n] for n in range(2)])
-
+                pairs(s - 1, rows, [spec.at[(s - 2) * 2 + n] for n in range(2)], [spec.at[(s - 1) * 2 + n] for n in range(2)])
+
+    hear(1)
+    tell(2)
     for n in range(2):
         for copy in copies[2 * n : 2 * n + 2]:
             copy.wait_recv()
@@ -344,7 +373,7 @@
             transform_rows(0, rows[k], n, k)
         for k, parts in enumerate(spectra(n)):
             keep(spec, rows[k], parts)
-        pairs(0, rows, [spec[i] for i in rows], [first_spec[i] for i in rows])
+        pairs(0, rows, [spec.at[i] for i in rows], [first_spec.at[i] for i in rows])
 
     lane8 = iota((8, LANES), 1)
     row8 = iota((8, LANES), 0)
@@ -481,7 +510,7 @@
         slot = pl.ds(n, 1)
         return remote(plane_sum.at[pl.ds(0, 1)], plane_sum.at[slot], sum_send, sum_recv, z_by_step[n])
 
-    z_by_step = [(z_ring[n] * X_COUNT + px, t) for n in range(z_count)]
+    hear(2)
     for n in sorted(range(1, z_count), key=lambda n: -hops(n, z_count)):
         to_z(n).start()
 
@@ -545,9 +574,9 @@
             pltpu.VMEM(constants.shape, bf16),
             pltpu.VMEM((SEC + 1, WIDE, COLS), bf16),
             pltpu.VMEM((SEC + 1, WIDE, COLS), bf16),
-            pltpu.VMEM((SEC + 1, 4 * PATCH, COLS), bf16),
-            pltpu.VMEM((2 * SEC, 4 * HALF, COLS), f32),
-            pltpu.VMEM((NODES, 4 * HALF, COLS), f32),
+            pltpu.VMEM((SEC + 1, 2, NODES * PATCH, COLS), bf16),
+            pltpu.VMEM((2 * SEC, 2, NODES, PATCH, LANES), f32),
+            pltpu.VMEM((NODES, 2, NODES, PATCH, LANES), f32),
             pltpu.VMEM((NODES, 2 * SEC, NODES * LANES), f32),
             pltpu.VMEM((NODES, 2 * SEC, NODES * LANES), f32),
             pltpu.VMEM((1, 2, LANES), f32),
@@ -560,6 +589,7 @@
             dma,
             dma,
             dma,
+            pltpu.SemaphoreType.REGULAR((3,)),
         ],
         compiler_params=pltpu.CompilerParams(
             collective_id=0, has_side_effects=True, vmem_limit_bytes=64 * 1024 * 1024 - 65536

time: 44.6 us -> 43.3 us (0.971)
  Pallas kernels: 41.8 us -> 40.5 us
    pallas_call x1, Pallas kernels: 41.8 us -> 40.5 us  [local(): pl.pallas_call(functools.partial(kernel, slabs, tiles), out_shape=(out, o...]
where the time goes in v4:
time: 43.3 us; the launch traced here: 43.1 us
  Pallas kernels  40.5 us (94%)
  local copies, waits for them, and re-layouts  1.94 us (4%)
  between operations  0.65 us (2%)
    pallas_call x1, Pallas kernels, local(): pl.pallas_call(functools.partial(kernel, slabs, tiles), out_shape=(out, o...  40.5 us
    unnamed x4, local copies, waits for them, and re-layouts  1.94 us

profile of v4, /device:TPU:1, one launch (start us, length us, event | category | flops | bytes accessed | tf_op | source)
XLA Modules:
  0.0 43.1 jit_solution(10241450534684159458)
XLA Ops:
  0.6 40.5 %shard_map.50 = (f32[2,4,4,4]{3,2,1,0:T(4,128)}, f32[2,4,4,4]{3,2,1,0:T(4,128)}) custom-call(f32[4,256,256]{2,1,0:T(8,128)} %images.1, s32[4,4,4]{2,1,0:T(4,128)} %mask_in.1, bf16[5,256,256]{2,1,0:T(8,128)(2,1)} %constant.2.clone.table_in), custom_call_target="tpu_custom_call" | custom-call | tf_op jit(solution)/shard_map/pallas_call | solution.py:566
  41.1 0.0 copy-start
  41.1 1.3 %copy.7 = f32[2,4,4,4]{3,2,1,0:T(4,128)} copy(f32[2,4,4,4]{3,2,1,0:T(4,128)} %get-tuple-element.4) | data formatting | bytes 1024
  42.5 0.0 copy-done
  42.5 0.6 %copy.8 = f32[2,4,4,4]{3,2,1,0:T(4,128)} copy(f32[2,4,4,4]{3,2,1,0:T(4,128)S(1)} %copy-done) | data formatting | bytes 1024
Async XLA Ops:
  41.1 1.3 %copy-start = (f32[2,4,4,4]{3,2,1,0:T(4,128)S(1)}, f32[2,4,4,4]{3,2,1,0:T(4,128)}, u32[]{:S(2)}) copy-start(f32[2,4,4,4]{3,2,1,0:T(4,128)} %get-tuple-element.5) | copy-start | bytes 1540

commit v5 on v4

--- a/solution.py
+++ b/solution.py
@@ -129,19 +129,22 @@
     steps.sort(key=lambda ab: -hops(ab[0], X_COUNT) - hops(ab[1], tiles) / 2)
     plane_mates = [(pz * X_COUNT + x_ring[a], t_ring[b]) for a, b in steps]
     z_by_step = [(z_ring[n] * X_COUNT + px, t) for n in range(z_count)]
-    near_z = [z_by_step[1 % z_count], z_by_step[z_count - 1]]
-    reaches = []
-    while 2 ** len(reaches) < z_count // 2:
-        reaches.append(2 ** len(reaches))
+    near = [(a, b) for a in (p_back, p, p_next) for b in (t_back, t, t_next)]
+    near.pop(4)
+    near += [z_by_step[1 % z_count], z_by_step[z_count - 1]]
+    p_ring = (lax.rem(p + slabs - 2, slabs), p, lax.rem(p + 2, slabs))
+    t_wide = (lax.rem(t + tiles - 2, tiles), t, lax.rem(t + 2, tiles))
+    wider = [(a, b) for a in p_ring for b in t_wide]
+    wider.pop(4)
+    wider += [z_by_step[2 % z_count], z_by_step[z_count - 2]]
+    rounds = [near, wider, [z_by_step[4 % z_count], z_by_step[z_count - 4]]]
 
     def tell(n):
-        if n < len(reaches):
-            for step in (reaches[n], z_count - reaches[n]):
-                pl.semaphore_signal(relay.at[n], inc=1, device_id=z_by_step[step], device_id_type=MESH)
+        for device in rounds[n]:
+            pl.semaphore_signal(relay.at[n], inc=1, device_id=device, device_id_type=MESH)
 
     def hear(n):
-        if n < len(reaches):
-            pl.semaphore_wait(relay.at[n], 2)
+        pl.semaphore_wait(relay.at[n], len(rounds[n]))
 
     def signal(device):
         pl.semaphore_signal(barrier, inc=1, device_id=device, device_id_type=MESH)
@@ -155,12 +158,7 @@
 
     barrier = pltpu.get_barrier_semaphore()
 
-    for device in near_z:
-        signal(device)
-    for n in range(tiles):
-        signal((z_back * X_COUNT + X_COUNT - 1, n))
-        signal((z_next * X_COUNT, n))
-    for device in plane_mates:
+    for device in near:
         signal(device)
 
     def remote(src, dst, send_sem, recv_sem, device):
@@ -317,11 +315,27 @@
             sums[i, pl.ds(earlier + SEC, 1), place] = moment
 
     def begin():
-        pl.semaphore_wait(barrier, plane - 1 + 2 + plane * jnp.where(at_low | at_high, 1, 0))
+        pl.semaphore_wait(barrier, len(near))
         for copy in copies:
             copy.start()
         tell(0)
 
+    lane8 = iota((8, LANES), 1)
+    row8 = iota((8, LANES), 0)
+    live = lax.rem(row8, SEC) + p > 0
+    own_mask.wait()
+    springs = jnp.zeros((8, LANES), f32)
+    for i in range(NODES):
+        here = jnp.concatenate([mask[s, i : i + 1, :] for s in range(SEC)], axis=0).astype(f32)
+        here = jnp.concatenate([here, jnp.zeros((SEC, LANES - NODES), f32)], axis=1)
+        here = jnp.concatenate([here, jnp.zeros((SEC, LANES), f32)], axis=0)
+        springs = springs + (pltpu.roll(here, i * NODES, 1) if i else here)
+    springs = jnp.where(live, springs, 0.0)
+
+    def flat(x):
+        return jnp.sum(pltpu.roll(x, 0, 1, stride=BLOCK, stride_axis=0), axis=0, keepdims=True)
+
+    outbox[0, 1:2, :] = flat(springs)
     own.wait()
     for s in range(1, SEC + 1):
         prepare(s, RIM, ROWS)
@@ -375,8 +389,6 @@
             keep(spec, rows[k], parts)
         pairs(0, rows, [spec.at[i] for i in rows], [first_spec.at[i] for i in rows])
 
-    lane8 = iota((8, LANES), 1)
-    row8 = iota((8, LANES), 0)
     lag_cols = jnp.where(lane8 < PATCH // 2, lane8, lane8 - PATCH).astype(f32)
     along = jnp.zeros((8, LANES), f32)
     across = jnp.zeros((8, LANES), f32)
@@ -388,26 +400,12 @@
             here = lane8 == i * NODES + j
             along = jnp.where(here, jnp.sum(scaled, axis=1, keepdims=True), along)
             across = jnp.where(here, jnp.sum(scaled * lag_cols, axis=1, keepdims=True), across)
-    live = lax.rem(row8, SEC) + p > 0
     low_half = row8 < SEC
     numerator = jnp.where(low_half, pltpu.roll(along, SEC, 0), pltpu.roll(across, SEC, 0))
     denominator = jnp.where(low_half, along, pltpu.roll(along, SEC, 0))
     flows = jnp.where(live & (lane8 < BLOCK), numerator / denominator, 0.0)
 
-    own_mask.wait()
-    springs = jnp.zeros((8, LANES), f32)
-    for i in range(NODES):
-        here = jnp.concatenate([mask[s, i : i + 1, :] for s in range(SEC)], axis=0).astype(f32)
-        here = jnp.concatenate([here, jnp.zeros((SEC, LANES - NODES), f32)], axis=1)
-        here = jnp.concatenate([here, jnp.zeros((SEC, LANES), f32)], axis=0)
-        springs = springs + (pltpu.roll(here, i * NODES, 1) if i else here)
-    springs = jnp.where(live, springs, 0.0)
-
-    def flat(x):
-        return jnp.sum(pltpu.roll(x, 0, 1, stride=BLOCK, stride_axis=0), axis=0, keepdims=True)
-
     outbox[0, 0:1, :] = flat(flows)
-    outbox[0, 1:2, :] = flat(springs)
     inbox[(1 + px) * tiles + t] = outbox[0]
 
     def give(q, sem, device):
@@ -424,6 +422,9 @@
                 for s in range(SEC):
                     out[c, s, i : i + 1, :] = moved[c * SEC + s : c * SEC + s + 1, :NODES]
 
+    for device in plane_mates:
+        give(1 + px, 0, device).start()
+
     @pl.when(at_high)
     def _():
         for x in range(X_COUNT):
@@ -436,8 +437,6 @@
             for n in range(tiles):
                 give(X_COUNT + 1, 1, (z_back * X_COUNT + x, n)).start()
 
-    for device in plane_mates:
-        give(1 + px, 0, device).start()
 
     write(flow_out, flows)
 
@@ -453,23 +452,26 @@
             x = jnp.where(row_bit == lane_bit, x, jnp.where(row_bit, down, up))
         return x
 
-    flow_parts, spring_parts = [], []
-    for q in range(X_COUNT + 2):
-        there = 1.0
+    def received(q, row):
+        x = inbox[q * tiles : (q + 1) * tiles, row, :]
+        if tiles < 8:
+            x = jnp.concatenate([x, jnp.zeros((8 - tiles, LANES), f32)], axis=0)
         if q == 0:
-            there = (pz > 0).astype(f32)
+            x = x * (pz > 0).astype(f32)
         elif q == X_COUNT + 1:
-            there = (pz < z_count - 1).astype(f32)
-        here = slice(q * tiles, (q + 1) * tiles)
-        flow_q, spring_q = inbox[here, 0, :], inbox[here, 1, :]
-        if tiles < 8:
-            pad = jnp.zeros((8 - tiles, LANES), f32)
-            flow_q, spring_q = (jnp.concatenate([v, pad], axis=0) for v in (flow_q, spring_q))
-        flow_parts.append(there * transpose_blocks(flow_q))
-        spring_parts.append(there * transpose_blocks(spring_q)[:SEC])
+            x = x * (pz < z_count - 1).astype(f32)
+        return x
+
+    flow_parts, spring_parts = ([], []), []
+    left8 = lane8 < HALF
+    for q in range(0, X_COUNT + 2, 2):
+        first, second = received(q, 0), received(q + 1, 0)
+        flow_parts[0].append(transpose_blocks(jnp.where(left8, first, pltpu.roll(second, HALF, 1))))
+        flow_parts[1].append(transpose_blocks(jnp.where(left8, pltpu.roll(first, HALF, 1), second)))
+        spring_parts.append(transpose_blocks(received(q, 1) + pltpu.roll(received(q + 1, 1), HALF, 1)))
     wide = (X_COUNT + 2) * SEC
     spring = jnp.concatenate(spring_parts, axis=0)
-    flow = [jnp.concatenate([v[c * SEC : (c + 1) * SEC] for v in flow_parts], axis=0) for c in range(2)]
+    flow = [jnp.concatenate(parts, axis=0) for parts in flow_parts]
     lane = iota((wide, LANES), 1)
     node_col = lax.rem(lane, NODES)
     live_lanes = (lane < tiles * BLOCK).astype(f32)
@@ -496,9 +498,11 @@
             chain.append(apply(chain[-1]))
         powers.append(chain)
     grams = [(a, b) for a in range(STEPS) for b in range(a, STEPS)]
-    core = slice(SEC, SEC + X_COUNT * SEC)
+    row = iota((wide, LANES), 0)
+    inner = ((row >= SEC) & (row < wide - SEC)).astype(f32)
+    inner_powers = [[v * inner for v in chain] for chain in powers]
     rows = [
-        jnp.sum(powers[0][a][core] * powers[0][b][core] + powers[1][a][core] * powers[1][b][core], axis=0, keepdims=True)
+        jnp.sum(inner_powers[0][a] * powers[0][b] + inner_powers[1][a] * powers[1][b], axis=0, keepdims=True)
         for a, b in grams
     ]
     totals = jnp.concatenate(rows + [jnp.zeros((16 - len(grams), LANES), f32)], axis=0)

time: 43.3 us -> 41.6 us (0.961)
  Pallas kernels: 40.5 us -> 38.8 us
    pallas_call x1, Pallas kernels: 40.5 us -> 38.8 us  [local(): pl.pallas_call(functools.partial(kernel, slabs, tiles), out_shape=(out, o...]
where the time goes in v5:
time: 41.6 us; the launch traced here: 41.4 us
  Pallas kernels  38.8 us (93%)
  local copies, waits for them, and re-layouts  1.94 us (5%)
  between operations  0.65 us (2%)
    pallas_call x1, Pallas kernels, local(): pl.pallas_call(functools.partial(kernel, slabs, tiles), out_shape=(out, o...  38.8 us
    unnamed x4, local copies, waits for them, and re-layouts  1.94 us

profile of v5, /device:TPU:1, one launch (start us, length us, event | category | flops | bytes accessed | tf_op | source)
XLA Modules:
  0.0 41.4 jit_solution(8440480061509682292)
XLA Ops:
  0.6 38.8 %shard_map.50 = (f32[2,4,4,4]{3,2,1,0:T(4,128)}, f32[2,4,4,4]{3,2,1,0:T(4,128)}) custom-call(f32[4,256,256]{2,1,0:T(8,128)} %images.1, s32[4,4,4]{2,1,0:T(4,128)} %mask_in.1, bf16[5,256,256]{2,1,0:T(8,128)(2,1)} %constant.2.clone.table_in), custom_call_target="tpu_custom_call" | custom-call | tf_op jit(solution)/shard_map/pallas_call | solution.py:570
  39.4 0.0 copy-start
  39.5 1.3 %copy.7 = f32[2,4,4,4]{3,2,1,0:T(4,128)} copy(f32[2,4,4,4]{3,2,1,0:T(4,128)} %get-tuple-element.4) | data formatting | bytes 1024
  40.8 0.0 copy-done
  40.8 0.6 %copy.8 = f32[2,4,4,4]{3,2,1,0:T(4,128)} copy(f32[2,4,4,4]{3,2,1,0:T(4,128)S(1)} %copy-done) | data formatting | bytes 1024
Async XLA Ops:
  39.4 1.3 %copy-start = (f32[2,4,4,4]{3,2,1,0:T(4,128)S(1)}, f32[2,4,4,4]{3,2,1,0:T(4,128)}, u32[]{:S(2)}) copy-start(f32[2,4,4,4]{3,2,1,0:T(4,128)} %get-tuple-element.5) | copy-start | bytes 1540

commit v6 on v5

--- a/solution.py
+++ b/solution.py
@@ -339,11 +339,11 @@
     own.wait()
     for s in range(1, SEC + 1):
         prepare(s, RIM, ROWS)
+    begin()
     first_tables.wait()
     for s in range(1, SEC + 1):
         for n in range(2):
             transform_rows(s, 1 + n, s, n)
-    begin()
     other_tables.wait()
 
     @pl.loop(0, 2)

time: 41.6 us -> 41.6 us (level)
  no operation moved by 1% of the time
where the time goes in v6:
time: 41.6 us; the launch traced here: 41.4 us
  Pallas kernels  38.8 us (93%)
  local copies, waits for them, and re-layouts  1.94 us (5%)
  between operations  0.65 us (2%)
    pallas_call x1, Pallas kernels, local(): pl.pallas_call(functools.partial(kernel, slabs, tiles), out_shape=(out, o...  38.8 us
    unnamed x4, local copies, waits for them, and re-layouts  1.94 us

profile of v6, /device:TPU:1, one launch (start us, length us, event | category | flops | bytes accessed | tf_op | source)
XLA Modules:
  0.0 41.4 jit_solution(16010214252085501764)
XLA Ops:
  0.6 38.8 %shard_map.50 = (f32[2,4,4,4]{3,2,1,0:T(4,128)}, f32[2,4,4,4]{3,2,1,0:T(4,128)}) custom-call(f32[4,256,256]{2,1,0:T(8,128)} %images.1, s32[4,4,4]{2,1,0:T(4,128)} %mask_in.1, bf16[5,256,256]{2,1,0:T(8,128)(2,1)} %constant.2.clone.table_in), custom_call_target="tpu_custom_call" | custom-call | tf_op jit(solution)/shard_map/pallas_call | solution.py:570
  39.4 0.0 copy-start
  39.5 1.3 %copy.7 = f32[2,4,4,4]{3,2,1,0:T(4,128)} copy(f32[2,4,4,4]{3,2,1,0:T(4,128)} %get-tuple-element.4) | data formatting | bytes 1024
  40.8 0.0 copy-done
  40.8 0.6 %copy.8 = f32[2,4,4,4]{3,2,1,0:T(4,128)} copy(f32[2,4,4,4]{3,2,1,0:T(4,128)S(1)} %copy-done) | data formatting | bytes 1024
Async XLA Ops:
  39.4 1.3 %copy-start = (f32[2,4,4,4]{3,2,1,0:T(4,128)S(1)}, f32[2,4,4,4]{3,2,1,0:T(4,128)}, u32[]{:S(2)}) copy-start(f32[2,4,4,4]{3,2,1,0:T(4,128)} %get-tuple-element.5) | copy-start | bytes 1540
